TPU v7x, 256 devices: a whole 4x4x8 slice. The times are simulated.
256 devices in a mesh: row: 16 (over x, y_lo, core), col: 16 (over z, y_hi).
Axes of the slice: x: 4, y: 4 (y_hi: 2, y_lo: 2; y = y_hi * 2 + y_lo), z: 8, core: 2. Of those that a mesh axis runs over, the one named last changes fastest.
Arguments:
- tokens: float32 [2048, 2048, 128], P('row', 'col'), may hold values from -6 to 6
- regions: int32 [2048, 2048], P('row', 'col'), may hold values from 0 to 15, as said below
- rel_index: int32 [64, 64], replicated, may hold values from 0 to 224, as said below
- bias_table: float32 [225, 4], replicated, may hold values from -215 to 215
- norm1_gain: float32 [128], replicated, may hold values from 0.1 to 1.9
- w_qkv: bfloat16 [128, 384], replicated, may hold values from -0.5 to 0.5
- w_proj: bfloat16 [128, 128], replicated, may hold values from -0.5 to 0.5
- norm2_gain: float32 [128], replicated, may hold values from 0.1 to 1.9
- w_up: bfloat16 [128, 512], replicated, may hold values from -0.5 to 0.5
- w_down: bfloat16 [512, 128], replicated, may hold values from -0.25 to 0.25
- merge_gain: float32 [512], replicated, may hold values from 0.1 to 1.9
- w_merge: bfloat16 [512, 256], replicated, may hold values from -0.25 to 0.25
Outputs:
- merged: bfloat16 [1024, 1024, 256], P('row', 'col')
Inputs may be any that keep to these rules, and one draw needn't show every extreme that they name: `regions`: constant on strips of 16 token rows and 16 token columns. `rel_index`: entries of one value belong to a single relative offset; every entry of the table is used.
All inputs are finite; a program needn't handle non-finite values.
Results may differ from a plain program's by a relative error of at most 0.011.
Values may be sent and summed in bfloat16 or wider, within the bound.
No kernel may reach another device: no remote copies, remote signals or barrier semaphores. Data moves between devices by JAX's collectives and lax.ppermute only.
A program may use at most 128 MiB of HBM per device.

v0:
```python
import jax
import jax.numpy as jnp
from jax import lax
from jax.sharding import PartitionSpec as P

C = 128
HEADS = 4
HD = 32
WIN = 8
SHIFT = 4


def from_behind(shard, axis, by):
    size = lax.axis_size(axis)
    return lax.ppermute(shard, axis, [(i, (i + by) % size) for i in range(size)])


def as_sent(shard):

    def short(part):
        return part.astype(jnp.bfloat16) if part.dtype == jnp.float32 else part

    return jax.tree.map(short, shard)


def layer_norm(values, gain):
    mean = jnp.mean(values, axis=-1, keepdims=True)
    centred = values - mean
    var = jnp.mean(centred * centred, axis=-1, keepdims=True)
    return centred / jnp.sqrt(var + 1e-05) * gain


def build_bias(rel_index, bias_table):
    entries = bias_table.shape[0]
    onehot = (rel_index[:, :, None] == jnp.arange(entries, dtype=jnp.int32)[None, None, :]).astype(
        jnp.float32
    )
    return jnp.einsum("ijt,th->hij", onehot, bias_table, precision=lax.Precision.HIGHEST)


def to_windows(field, side):
    blocks = side // WIN
    if field.ndim == 3:
        split = field.reshape(blocks, WIN, blocks, WIN, field.shape[2]).swapaxes(1, 2)
        return split.reshape(blocks, blocks, WIN * WIN, field.shape[2])
    split = field.reshape(blocks, WIN, blocks, WIN).swapaxes(1, 2)
    return split.reshape(blocks, blocks, WIN * WIN)


def from_windows(windows, side):
    blocks = side // WIN
    joined = windows.reshape(blocks, blocks, WIN, WIN, C).swapaxes(1, 2)
    return joined.reshape(side, side, C)


def attend_row(
    win_in, win_ids, bias, headmask, norm1_gain, w_qkv, w_proj, norm2_gain, w_up, w_down
):
    count = win_in.shape[0]
    spots = WIN * WIN
    flat = win_in.reshape(count * spots, C)
    normed = layer_norm(flat, norm1_gain).astype(jnp.bfloat16)
    qkv = jnp.dot(normed, w_qkv, preferred_element_type=jnp.float32).astype(jnp.bfloat16)
    query = qkv[:, :C].reshape(count, spots, C)
    keys = qkv[:, C : 2 * C].reshape(count, spots, C)
    values = qkv[:, 2 * C :].reshape(count, spots, C)
    masked = query[:, None] * headmask[None, :, None, :]
    scores = (
        jnp.einsum("whqc,wkc->whqk", masked, keys, preferred_element_type=jnp.float32)
        * HD ** (-0.5)
        + bias[None]
    )
    same = win_ids[:, :, None] == win_ids[:, None, :]
    scores = jnp.where(same[:, None], scores, -1e30)
    top = jnp.max(scores, axis=-1, keepdims=True)
    expo = jnp.exp(scores - top)
    probs = (expo / jnp.sum(expo, axis=-1, keepdims=True)).astype(jnp.bfloat16)
    per_head = jnp.einsum("whqk,wkc->whqc", probs, values, preferred_element_type=jnp.float32)
    attended = jnp.sum(per_head * headmask[None, :, None, :].astype(jnp.float32), axis=1)
    attended = attended.astype(jnp.bfloat16).reshape(count * spots, C)
    projected = jnp.dot(attended, w_proj, preferred_element_type=jnp.float32)
    middle = flat + projected
    second = layer_norm(middle, norm2_gain).astype(jnp.bfloat16)
    widened = jax.nn.gelu(jnp.dot(second, w_up, preferred_element_type=jnp.float32)).astype(
        jnp.bfloat16
    )
    down = jnp.dot(widened, w_down, preferred_element_type=jnp.float32)
    return (middle + down).reshape(count, spots, C)


def merge_patches(block, merge_gain, w_merge):
    joined = jnp.concatenate(
        [block[0::2, 0::2], block[1::2, 0::2], block[0::2, 1::2], block[1::2, 1::2]], axis=-1
    )
    normed = layer_norm(joined, merge_gain).astype(jnp.bfloat16)
    rows_out, cols_out = (normed.shape[0], normed.shape[1])
    out = jnp.dot(
        normed.reshape(rows_out * cols_out, 4 * C), w_merge, preferred_element_type=jnp.float32
    )
    return out.astype(jnp.bfloat16).reshape(rows_out, cols_out, 2 * C)


def on_device(
    tokens,
    regions,
    rel_index,
    bias_table,
    norm1_gain,
    w_qkv,
    w_proj,
    norm2_gain,
    w_up,
    w_down,
    merge_gain,
    w_merge,
):
    side = tokens.shape[0]
    below, below_ids = (
        from_behind(tokens[:SHIFT].astype(jnp.bfloat16), "row", -1).astype(jnp.float32),
        from_behind(regions[:SHIFT], "row", -1),
    )
    band = jnp.concatenate([tokens[SHIFT:, :SHIFT], below[:, :SHIFT]], axis=0)
    band_ids = jnp.concatenate([regions[SHIFT:, :SHIFT], below_ids[:, :SHIFT]], axis=0)
    right, right_ids = (
        from_behind(band.astype(jnp.bfloat16), "col", -1).astype(band.dtype),
        from_behind(band_ids, "col", -1),
    )
    shifted = jnp.concatenate(
        [
            jnp.concatenate([tokens[SHIFT:, SHIFT:], right[: side - SHIFT]], axis=1),
            jnp.concatenate([below[:, SHIFT:], right[side - SHIFT :]], axis=1),
        ],
        axis=0,
    )
    shifted_ids = jnp.concatenate(
        [
            jnp.concatenate([regions[SHIFT:, SHIFT:], right_ids[: side - SHIFT]], axis=1),
            jnp.concatenate([below_ids[:, SHIFT:], right_ids[side - SHIFT :]], axis=1),
        ],
        axis=0,
    )
    windows = to_windows(shifted, side)
    window_ids = to_windows(shifted_ids, side)
    bias = build_bias(rel_index, bias_table)
    headmask = (
        jnp.arange(C, dtype=jnp.int32)[None, :] // HD == jnp.arange(HEADS, dtype=jnp.int32)[:, None]
    ).astype(jnp.bfloat16)

    def run_block(pair):
        return attend_row(
            pair[0], pair[1], bias, headmask, norm1_gain, w_qkv, w_proj, norm2_gain, w_up, w_down
        )

    block_out = from_windows(lax.map(run_block, (windows, window_ids)), side)
    above = from_behind(as_sent(block_out[side - SHIFT :]), "row", 1)
    band_back = jnp.concatenate(
        [above[:, side - SHIFT :], block_out[: side - SHIFT, side - SHIFT :]], axis=0
    )
    leftward = from_behind(as_sent(band_back), "col", 1).astype(band_back.dtype)
    restored = jnp.concatenate(
        [
            jnp.concatenate([leftward[:SHIFT], above[:, : side - SHIFT]], axis=1),
            jnp.concatenate([leftward[SHIFT:], block_out[: side - SHIFT, : side - SHIFT]], axis=1),
        ],
        axis=0,
    )
    merged = merge_patches(restored, merge_gain, w_merge)
    return merged


def solution(mesh):
    return jax.shard_map(
        on_device,
        mesh=mesh,
        in_specs=(
            P("row", "col", None),
            P("row", "col"),
            P(),
            P(),
            P(),
            P(),
            P(),
            P(),
            P(),
            P(),
            P(),
            P(),
        ),
        out_specs=P("row", "col", None),
        check_vma=False,
    )
```

profile of v0, /device:TPU:0, one launch (start us, length us, event | category | flops | bytes accessed | tf_op | source)
XLA Modules:
  0.0 384.8 jit_solution(9834371594216935121)
XLA Ops:
  0.0 4.4 %convert.14 = bf16[128,128,128]{2,1,0:T(8,128)(2,1)S(1)} convert(f32[128,128,128]{2,1,0:T(8,128)} %param.14) | non-fusion elementwise | flops 2097152 | bytes 12582912 | tf_op jit(solution)/shard_map/convert.7
  8.8 2.8 fusion.57
  11.8 8.2 %collective-permute-start.3 = (s32[128,4]{0,1:T(4,128)S(1)}, s32[128,4]{0,1:T(4,128)S(1)}, u32[]{:S(2)}, u32[]{:S(2)}) collective-permute-start(s32[128,4]{0,1:T(4,128)S(1)} %pad_add_fusion), channel_id=1, source_target_pairs={{0,15},{1,0},{2,1},{3,2},{4,3},{5,4},{6,5},{7,6},{8,7},{9,8},{10,9... | collective-permute-start | bytes 6152 | tf_op jit(solution)/shard_map/ppermute | solution.py:15
  21.0 8.3 %slice.92 = f32[124,124,128]{2,1,0:T(8,128)} slice(f32[128,128,128]{2,1,0:T(8,128)} %param.14), slice={[4:128], [4:128], [0:128]} | slice | bytes 15745024 | tf_op jit(solution)/shard_map/slice | solution.py:130
  32.1 5.8 %collective-permute-done.1 = bf16[128,4,128]{2,1,0:T(4,128)(2,1)S(1)} collective-permute-done((bf16[128,4,128]{2,1,0:T(4,128)(2,1)S(1)}, bf16[128,4,128]{2,1,0:T(4,128)(2,1)S(1)}, u32[]{:S(2)}, u32[]{:S(2)}) %collective-permute-start.1) | collective-permute-done | bytes 131104 | tf_op jit(solution)/shard_map/ppermute | solution.py:15
  38.0 7.4 %maximum_maximum_fusion = f32[128,128,128]{2,1,0:T(8,128)S(1)} fusion(f32[4,4,128]{2,1,0:T(4,128)S(1)} %slice.132, f32[4,124,128]{2,1,0:T(8,128)S(1)} %slice_convert_fusion.1, f32[124,4,128]{2,1,0:T(4,128)S(1)} %slice.130, f32[124,124,128]{2,1,0:T(8,128)} %slice.92), kind=kLoop, calls=%fused_computation.59 | loop fusion | flops 6291456 | bytes 16777216 | tf_op jit(solution)/shard_map/concatenate | solution.py:128
  45.4 4.4 %copy.54 = f32[16,8,16,8,128]{4,3,1,2,0:T(8,128)} copy(f32[16,8,16,8,128]{4,3,2,1,0:T(8,128)S(1)} %bitcast.90) | data formatting | bytes 16777216 | tf_op jit(solution)/shard_map/reshape | solution.py:44
  49.9 164.4 %while.12 = (s32[]{:T(128)}, f32[16,16,64,128]{3,2,1,0:T(8,128)}, f32[16,16,64,128]{3,2,1,0:T(8,128)}, s32[16,16,64]{2,1,0:T(8,128)S(1)}, f32[128]{0:T(128)S(1)}...) while((s32[]{:T(128)}, f32[16,16,64,128]{3,2,1,0:T(8,128)}, ...), condition=%wide.region_8.9_spmd.clone.clone, body=%wide.region_0.8_spmd.clone.clone.sunk | while | flops 547688000 | bytes 12791941 | solution.py:154
  52.8 2.5 fusion.104
  63.1 2.5 fusion.104
  73.5 2.5 fusion.104
  83.7 2.5 fusion.104
  104.3 2.5 fusion.104
  114.5 2.5 fusion.104
  124.8 2.5 fusion.104
  135.0 2.5 fusion.104
  145.3 2.5 fusion.104
  155.6 2.5 fusion.104
  165.9 2.5 fusion.104
  176.1 2.5 fusion.104
  186.4 2.5 fusion.104
  196.7 2.5 fusion.104
  214.3 4.5 %copy.48 = f32[16,8,16,8,128]{4,3,2,1,0:T(8,128)S(1)} copy(f32[16,8,16,8,128]{4,3,1,2,0:T(8,128)} %bitcast.97) | data formatting | bytes 16777216 | tf_op jit(solution)/shard_map/transpose | solution.py:52
  221.1 5.5 %collective-permute-done.4 = bf16[4,128,128]{2,1,0:T(8,128)(2,1)S(1)} collective-permute-done((bf16[4,128,128]{2,1,0:T(8,128)(2,1)S(1)}, bf16[4,128,128]{2,1,0:T(8,128)(2,1)S(1)}, u32[]{:S(2)}, u32[]{:S(2)}) %collective-permute-start.4) | collective-permute-done | bytes 131104 | tf_op jit(solution)/shard_map/ppermute | solution.py:15
  227.0 8.5 %collective-permute-done.5 = bf16[128,4,128]{2,1,0:T(4,128)(2,1)S(1)} collective-permute-done((bf16[128,4,128]{2,1,0:T(4,128)(2,1)S(1)}, bf16[128,4,128]{2,1,0:T(4,128)(2,1)S(1)}, u32[]{:S(2)}, u32[]{:S(2)}) %collective-permute-start.5) | collective-permute-done | bytes 131104 | tf_op jit(solution)/shard_map/ppermute | solution.py:15
  235.5 4.0 %maximum_maximum_fusion.1 = f32[128,128,128]{2,1,0:T(8,128)} fusion(f32[124,124,128]{2,1,0:T(8,128)S(1)} %slice.141, f32[124,4,128]{2,1,0:T(4,128)S(1)} %slice.140, f32[4,124,128]{2,1,0:T(8,128)S(1)} %slice_convert_fusion, f32[4,4,128]{2,1,0:T(4,128)S(1)} %slice.138), kind=kLoop, calls=%fused_computation.60 | loop fusion | flops 6291456 | bytes 16777216 | tf_op jit(solution)/shard_map/concatenate | solution.py:160
  239.5 29.5 %slice.114 = f32[64,64,128]{2,1,0:T(8,128)S(1)} slice(f32[128,128,128]{2,1,0:T(8,128)} %maximum_maximum_fusion.1), slice={[0:128:2], [0:128:2], [0:128:1]} | slice | bytes 4194304 | tf_op jit(solution)/shard_map/slice | solution.py:93
  269.0 33.4 %slice.115 = f32[64,64,128]{2,1,0:T(8,128)} slice(f32[128,128,128]{2,1,0:T(8,128)} %maximum_maximum_fusion.1), slice={[1:128:2], [0:128:2], [0:128:1]} | slice | bytes 4194304 | tf_op jit(solution)/shard_map/slice | solution.py:93
  302.4 33.4 %slice.116 = f32[64,64,128]{2,1,0:T(8,128)} slice(f32[128,128,128]{2,1,0:T(8,128)} %maximum_maximum_fusion.1), slice={[0:128:2], [1:128:2], [0:128:1]} | slice | bytes 4194304 | tf_op jit(solution)/shard_map/slice | solution.py:93
  335.8 33.4 %slice.117 = f32[64,64,128]{2,1,0:T(8,128)} slice(f32[128,128,128]{2,1,0:T(8,128)} %maximum_maximum_fusion.1), slice={[1:128:2], [1:128:2], [0:128:1]} | slice | bytes 4194304 | tf_op jit(solution)/shard_map/slice | solution.py:93
  376.4 3.5 fusion.52
  380.2 4.6 %convolution_convert_fusion.1 = bf16[4096,256]{1,0:T(8,128)(2,1)} fusion(bf16[512,256]{1,0:T(8,128)(2,1)S(1)} %copy-done, f32[4096,128]{1,0:T(8,128)} %bitcast.94, f32[4096,128]{1,0:T(8,128)} %bitcast.93, f32[4096,128]{1,0:T(8,128)} %bitcast.92, f32[4096,128]{1,0:T(8,128)S(1)} %bitcast.91, f32[512]{0:T(512)S(1)} %copy-done.10, f32[4096]{0:T(1024)S(1)} %sqrt.31, ...), kind=kOutput, calls=%fused_computation.69 | convolution fusion | flops 1089470464 | bytes 10782720 | tf_op jit(solution)/shard_map/dot_general | solution.py:97
  (382 shorter events, 145.8 us)
Async XLA Ops:
  0.0 380.2 %copy-start = (bf16[512,256]{1,0:T(8,128)(2,1)S(1)}, bf16[512,256]{1,0:T(8,128)(2,1)}, u32[]{:S(2)}) copy-start(bf16[512,256]{1,0:T(8,128)(2,1)} %param.25) | copy-start | bytes 786436
  0.0 7.9 %slice-start = ((s32[128,128]{1,0:T(8,128)}), s32[4,128]{1,0:T(4,128)S(1)}, s32[]{:S(2)}) async-start(s32[128,128]{1,0:T(8,128)} %param.15), calls=%async_computation | async-start | bytes 4096 | tf_op jit(solution)/shard_map/slice | solution.py:120
  0.0 11.6 %copy-start.4 = (s32[128,128]{1,0:T(8,128)S(1)}, s32[128,128]{1,0:T(8,128)}, u32[]{:S(2)}) copy-start(s32[128,128]{1,0:T(8,128)} %param.15) | copy-start | bytes 196612
  0.0 8.8 %copy-start.8 = (s32[64,64]{1,0:T(8,128)S(1)}, s32[64,64]{1,0:T(8,128)}, u32[]{:S(2)}) copy-start(s32[64,64]{1,0:T(8,128)} %param.16) | copy-start | bytes 49156
  0.0 8.8 %copy-start.9 = (f32[225,4]{0,1:T(4,128)S(1)}, f32[225,4]{0,1:T(4,128)}, u32[]{:S(2)}) copy-start(f32[225,4]{0,1:T(4,128)} %param.17) | copy-start | bytes 10804
  4.4 1.9 copy-start.1
  6.4 24.7 %collective-permute-start = (bf16[4,128,128]{2,1,0:T(8,128)(2,1)S(1)}, bf16[4,128,128]{2,1,0:T(8,128)(2,1)S(1)}, u32[]{:S(2)}, u32[]{:S(2)}) collective-permute-start(bf16[4,128,128]{2,1,0:T(8,128)(2,1)S(1)} %slice.128), channel_id=1, source_target_pairs={{0,240},{16,0},{32,16},{48,32},{64,48},{80,64},{96,80},{112,96},{1... | collective-permute-start | bytes 393224 | tf_op jit(solution)/shard_map/ppermute | solution.py:15
  8.0 3.7 collective-permute-start.2
  11.8 17.8 %collective-permute-start.3 = (s32[128,4]{0,1:T(4,128)S(1)}, s32[128,4]{0,1:T(4,128)S(1)}, u32[]{:S(2)}, u32[]{:S(2)}) collective-permute-start(s32[128,4]{0,1:T(4,128)S(1)} %pad_add_fusion), channel_id=1, source_target_pairs={{0,15},{1,0},{2,1},{3,2},{4,3},{5,4},{6,5},{7,6},{8,7},{9,8},{10,9... | collective-permute-start | bytes 6152 | tf_op jit(solution)/shard_map/ppermute | solution.py:15
  31.2 6.7 %collective-permute-start.1 = (bf16[128,4,128]{2,1,0:T(4,128)(2,1)S(1)}, bf16[128,4,128]{2,1,0:T(4,128)(2,1)S(1)}, u32[]{:S(2)}, u32[]{:S(2)}) collective-permute-start(bf16[128,4,128]{2,1,0:T(4,128)(2,1)S(1)} %pad_maximum_fusion), channel_id=1, source_target_pairs={{0,15},{1,0},{2,1},{3,2},{4,3},{5,4},{6,5},{7,6},{8,7},{9,8},{10,9... | collective-permute-start | bytes 393224 | tf_op jit(solution)/shard_map/ppermute | solution.py:15
  45.4 4.5 %copy-start.2 = (bf16[128,384]{1,0:T(8,128)(2,1)S(1)}, bf16[128,384]{1,0:T(8,128)(2,1)}, u32[]{:S(2)}) copy-start(bf16[128,384]{1,0:T(8,128)(2,1)} %param.19) | copy-start | bytes 294916
  45.4 4.5 %copy-start.3 = (bf16[128,128]{1,0:T(8,128)(2,1)S(1)}, bf16[128,128]{1,0:T(8,128)(2,1)}, u32[]{:S(2)}) copy-start(bf16[128,128]{1,0:T(8,128)(2,1)} %param.20) | copy-start | bytes 98308
  45.4 4.5 %copy-start.5 = (f32[128]{0:T(128)S(1)}, f32[128]{0:T(128)}, u32[]{:S(2)}) copy-start(f32[128]{0:T(128)} %param.18) | copy-start | bytes 1540
  45.4 4.5 %copy-start.6 = (bf16[128,512]{1,0:T(8,128)(2,1)S(1)}, bf16[128,512]{1,0:T(8,128)(2,1)}, u32[]{:S(2)}) copy-start(bf16[128,512]{1,0:T(8,128)(2,1)} %param.22) | copy-start | bytes 393220
  45.4 4.5 %copy-start.7 = (bf16[512,128]{1,0:T(8,128)(2,1)S(1)}, bf16[512,128]{1,0:T(8,128)(2,1)}, u32[]{:S(2)}) copy-start(bf16[512,128]{1,0:T(8,128)(2,1)} %param.23) | copy-start | bytes 393220
  45.4 4.5 %copy-start.11 = (f32[128]{0:T(128)S(1)}, f32[128]{0:T(128)}, u32[]{:S(2)}) copy-start(f32[128]{0:T(128)} %param.21) | copy-start | bytes 1540
  219.8 6.7 %collective-permute-start.4 = (bf16[4,128,128]{2,1,0:T(8,128)(2,1)S(1)}, bf16[4,128,128]{2,1,0:T(8,128)(2,1)S(1)}, u32[]{:S(2)}, u32[]{:S(2)}) collective-permute-start(bf16[4,128,128]{2,1,0:T(8,128)(2,1)S(1)} %slice.135), channel_id=1, source_target_pairs={{0,16},{16,32},{32,48},{48,64},{64,80},{80,96},{96,112},{112,128},... | collective-permute-start | bytes 393224 | tf_op jit(solution)/shard_map/ppermute | solution.py:15
  226.6 8.9 %collective-permute-start.5 = (bf16[128,4,128]{2,1,0:T(4,128)(2,1)S(1)}, bf16[128,4,128]{2,1,0:T(4,128)(2,1)S(1)}, u32[]{:S(2)}, u32[]{:S(2)}) collective-permute-start(bf16[128,4,128]{2,1,0:T(4,128)(2,1)S(1)} %pad_maximum_fusion.1), channel_id=1, source_target_pairs={{0,1},{1,2},{2,3},{3,4},{4,5},{5,6},{6,7},{7,8},{8,9},{9,10},{10,1... | collective-permute-start | bytes 393224 | tf_op jit(solution)/shard_map/ppermute | solution.py:15
  376.4 3.7 copy-start.10
where the time goes:
time: 390 us; the launch traced here: 385 us
  local copies, waits for them, and re-layouts  171 us (44%)
  matrix products  111 us (28%)
  other arithmetic  69.2 us (18%)
  waiting for transfers between devices  19.8 us (5%)
  starting transfers between devices  11.8 us (3%)
    sub x16, matrix products, attend_row(): expo = jnp.exp(scores - top)  40.3 us
    dot_general x16, matrix products, attend_row(): jnp.einsum('whqk,wkc->whqc', probs, values, preferred_element_type=jnp.fl...  33.7 us
    slice x1, local copies, waits for them, and re-layouts, merge_patches(): block[0::2, 1::2]  33.4 us
    slice x1, local copies, waits for them, and re-layouts, merge_patches(): block[1::2, 0::2]  33.4 us
    slice x1, local copies, waits for them, and re-layouts, merge_patches(): block[1::2, 1::2]  33.4 us
    slice x1, local copies, waits for them, and re-layouts, merge_patches(): block[0::2, 0::2]  29.5 us
    reduce_sum x20, other arithmetic, layer_norm(): mean = jnp.mean(values, axis=-1, keepdims=True)  27.2 us
    ppermute x6, waiting for transfers between devices, from_behind(): lax.ppermute(shard, axis, [(i, (i + by) % size) for i in range(size)])  19.8 us
  transfers between devices with their start and end apart: 6, of which 3 were waited for; matrix products, arithmetic and copies ran while one was open for 4% of the time, Pallas kernels for 0%

commit v1 on v0

v1 whole, which is shorter than its diff:
```python
import functools

import jax
import jax.numpy as jnp
from jax import lax
from jax.experimental import pallas as pl
from jax.experimental.pallas import tpu as pltpu
from jax.sharding import PartitionSpec as P

C = 128
HEADS = 4
HD = 32
WIN = 8
SPOTS = WIN * WIN
MLP = 512
SIDE = 128
OUT = SIDE // 2
STRIPS = SIDE // 16
IDROWS = 16
LOG2E = 1.4426950408889634
QSCALE = HD ** (-0.5) * LOG2E
VARIANTS = 24
F32 = jnp.float32
BF16 = jnp.bfloat16
NT = (((1,), (1,)), ((), ()))
TN = (((0,), (0,)), ((), ()))


def layer_norm(values, gain):
    mean = jnp.mean(values, axis=-1, keepdims=True)
    centred = values - mean
    var = jnp.mean(centred * centred, axis=-1, keepdims=True)
    return centred * lax.rsqrt(var + 1e-05) * gain


def half_gelu(half):
    h = half.astype(BF16)
    c0 = jnp.asarray(2.0 * 0.7978845608028654, BF16)
    c1 = jnp.asarray(8.0 * 0.7978845608028654 * 0.044715, BF16)
    inner = h * (c0 + c1 * (h * h))
    return h + h * jnp.tanh(inner)


def prepare(rel_ref, table_ref, w_qkv_ref, w_up_ref, bias_scr, wvt_scr, wup_scr, pad_scr):
    wvt_scr[...] = w_qkv_ref[:, 2 * C :].astype(F32).T.astype(BF16)
    wup_scr[...] = w_up_ref[...] * jnp.asarray(0.5, BF16)
    pad_scr[...] = jnp.zeros_like(pad_scr)
    pad_scr[pl.ds(0, table_ref.shape[0]), pl.ds(0, HEADS)] = table_ref[...]
    table_a = pad_scr[pl.ds(0, 128), :].T
    table_b = pad_scr[pl.ds(128, 128), :].T
    pad_scr[pl.ds(0, SPOTS), pl.ds(0, SPOTS)] = rel_ref[...].astype(F32)
    rel_t = pad_scr[pl.ds(0, 128), :].T[:SPOTS, :].astype(jnp.int32)
    rel_t = jnp.where(lax.broadcasted_iota(jnp.int32, (SPOTS, 128), 1) < SPOTS, rel_t, pltpu.roll(rel_t, SPOTS, 1))
    low = rel_t < 128
    spot = jnp.where(low, rel_t, rel_t - 128)
    lane = lax.broadcasted_iota(jnp.int32, (SPOTS, 128), 1)
    halves = []
    for pair in range(HEADS // 2):
        per_head = []
        for head in (2 * pair, 2 * pair + 1):
            row_a = jnp.broadcast_to(table_a[head : head + 1, :], (SPOTS, 128))
            row_b = jnp.broadcast_to(table_b[head : head + 1, :], (SPOTS, 128))
            got_a = jnp.take_along_axis(row_a, spot, axis=1, mode="promise_in_bounds")
            got_b = jnp.take_along_axis(row_b, spot, axis=1, mode="promise_in_bounds")
            per_head.append(jnp.where(low, got_a, got_b))
        halves.append(jnp.where(lane < SPOTS, per_head[0], per_head[1]) * LOG2E)
    bias = jnp.concatenate(halves, axis=1)
    key_spot = lax.broadcasted_iota(jnp.int32, (SPOTS, 2 * 128), 0)
    query_spot = lax.broadcasted_iota(jnp.int32, (SPOTS, 2 * 128), 1) % SPOTS

    def label_of(spots, labels):
        right = (spots % WIN) >= WIN // 2
        lower = spots >= SPOTS // 2
        top = jnp.where(right, labels[0], 0)
        low_row = jnp.where(right, labels[2], labels[1])
        return jnp.where(lower, low_row, top)

    def variant(index, carry):
        labels = (index // 12, (index // 4) % 3, index % 4)
        same = label_of(key_spot, labels) == label_of(query_spot, labels)
        bias_scr[index] = jnp.where(same, bias, -1e30)
        return carry

    lax.fori_loop(0, VARIANTS, variant, 0)


def pattern(top_left, top_right, low_left, low_right):
    one = jnp.where(top_right == top_left, 0, 1)
    two = jnp.where(low_left == top_left, 0, jnp.where(low_left == top_right, 1, 2))
    three = jnp.where(
        low_right == top_left,
        0,
        jnp.where(low_right == top_right, 1, jnp.where(low_right == low_left, 2, 3)),
    )
    return one * 12 + two * 4 + three


def front(loads, store_att, variants, w, bias_scr, wvt_scr):
    normed = []
    for load in loads:
        normed.append(layer_norm(load(), w["g1"][...]).astype(BF16))
        yield
    normed = jnp.concatenate(normed, axis=0)
    qk = jnp.dot(normed, w["w_qkv"][:, : 2 * C], preferred_element_type=F32)
    vt = lax.dot_general(wvt_scr[...], normed, NT, preferred_element_type=F32).astype(BF16)
    yield
    lane = lax.broadcasted_iota(jnp.int32, (1, C), 1)
    n = len(loads)
    st, ot = {}, {}
    for i in range(n + 2 * LAG):
        if i < n:
            rows = slice(SPOTS * i, SPOTS * (i + 1))
            q = (qk[rows, :C] * QSCALE).astype(BF16)
            k = qk[rows, C:].astype(BF16)
            qm = jnp.concatenate([jnp.where(lane // HD == h, q, jnp.zeros_like(q)) for h in range(HEADS)], axis=0)
            st[i] = lax.dot_general(k, qm, NT, preferred_element_type=F32)
        at = i - LAG
        if 0 <= at < n:
            rows = slice(SPOTS * at, SPOTS * (at + 1))
            scores = st.pop(at) + bias_scr[variants[at]]
            top = jnp.max(scores, axis=0, keepdims=True)
            p = jnp.exp2((scores - top).astype(BF16))
            vw = jnp.concatenate([vt[:, rows], jnp.ones((16, SPOTS), BF16)], axis=0)
            ot[at] = jnp.dot(vw, p, preferred_element_type=F32)
        at = i - 2 * LAG
        if 0 <= at < n:
            got = ot.pop(at)
            inv = 1.0 / got[C : C + 1]
            store_att(
                at,
                jnp.concatenate(
                    [
                        got[HD * h : HD * (h + 1), SPOTS * h : SPOTS * (h + 1)]
                        * inv[:, SPOTS * h : SPOTS * (h + 1)]
                        for h in range(HEADS)
                    ],
                    axis=0,
                ).astype(BF16),
            )
        yield


def back(loads, load_att, stores, w, wup_scr):
    proj = lax.dot_general(load_att(), w["w_proj"][...], TN, preferred_element_type=F32)
    yield
    mids, second = [], []
    for i, load in enumerate(loads):
        mids.append(load() + proj[SPOTS * i : SPOTS * (i + 1)])
        second.append(layer_norm(mids[-1], w["g2"][...]).astype(BF16))
        yield
    up = jnp.dot(jnp.concatenate(second, axis=0), wup_scr[...], preferred_element_type=F32)
    yield
    wide = []
    for i in range(len(loads)):
        wide.append(half_gelu(up[SPOTS * i : SPOTS * (i + 1)]))
        yield
    down = jnp.dot(jnp.concatenate(wide, axis=0), w["w_down"][...], preferred_element_type=F32)
    yield
    for i, store in enumerate(stores):
        store(mids[i] + down[SPOTS * i : SPOTS * (i + 1)])
        yield


LAG = 2


def merge(load_parts, store, w):
    joined = jnp.concatenate(load_parts(), axis=1)
    normed = layer_norm(joined, w["gm"][...]).astype(BF16)
    yield
    out = jnp.dot(normed, w["w_merge"][...], preferred_element_type=F32)
    yield
    store(out.astype(BF16))


def drive(timed):
    events = []
    for number, (start, gap, gen) in enumerate(timed):
        for step in range(80):
            events.append((start + gap * step, number, gen))
    for _, _, gen in sorted(events, key=lambda e: (e[0], e[1])):
        next(gen, None)


NAMES = ("g1", "w_qkv", "w_proj", "g2", "w_up", "w_down", "gm", "w_merge")
GROUP = 8
FRONT_EVERY, FRONT_GAP = 20, 1
BACK_EVERY, BACK_GAP = 16, 0.8
MERGE_EVERY, MERGE_GAP, MERGE_AT = 1.0, 1.0, 50


def interior_kernel(x_ref, old_ref, ids_ref, rel_ref, table_ref, *refs):
    w = dict(zip(NAMES, refs[:8]))
    out_ref, bias_scr, wvt_scr, wup_scr, pad_scr, att_scr, blk_scr = refs[8:]
    step = pl.program_id(0)
    count = SIDE // WIN - 1

    @pl.when(step == 0)
    def _():
        prepare(rel_ref, table_ref, w["w_qkv"], w["w_up"], bias_scr, wvt_scr, wup_scr, pad_scr)
        blk_scr[...] = jnp.zeros_like(blk_scr)

    upper, lower = step // 2, (step + 1) // 2

    def loader(ref, j):
        return lambda: jnp.concatenate([ref[y, pl.ds(WIN * j + 4, WIN), :] for y in range(WIN)], axis=0)

    def variant(j):
        left, right = 16 * (j // 2), 16 * ((j + 1) // 2)
        return pattern(ids_ref[upper, left], ids_ref[upper, right], ids_ref[lower, left], ids_ref[lower, right])

    def store_att(g):
        def store(i, value):
            att_scr[g, :, pl.ds(SPOTS * i, SPOTS)] = value

        return store

    def store_block(j):
        def store(value):
            for y in range(WIN):
                blk_scr[y, pl.ds(WIN * j + 4, WIN), :] = value[WIN * y : WIN * (y + 1)]

        return store

    groups = [list(range(at, min(at + GROUP, count))) for at in range(0, count, GROUP)]

    def fronts():
        return [
            (
                FRONT_EVERY * g,
                FRONT_GAP,
                front([loader(x_ref, j) for j in js], store_att(g), [variant(j) for j in js], w, bias_scr, wvt_scr),
            )
            for g, js in enumerate(groups)
        ]

    def backs():
        return [
            (
                BACK_EVERY * g,
                BACK_GAP,
                back(
                    [loader(old_ref, j) for j in js],
                    lambda g=g, js=js: att_scr[g, :, : SPOTS * len(js)],
                    [store_block(j) for j in js],
                    w,
                    wup_scr,
                ),
            )
            for g, js in enumerate(groups)
        ]

    def merges():
        def parts(a):
            return lambda: [blk_scr[2 * a + dy, pl.ds(dx, OUT, stride=2), :] for dx in range(2) for dy in range(2)]

        def store(a):
            def put(value):
                out_ref[a] = value

            return put

        return [(MERGE_AT + MERGE_EVERY * a, MERGE_GAP, merge(parts(a), store(a), w)) for a in range(4)]

    @pl.when(step == 0)
    def _():
        drive(fronts())

    @pl.when((step > 0) & (step < count))
    def _():
        drive(backs() + fronts() + merges())

    @pl.when(step == count)
    def _():
        drive(backs() + merges())


def whole(shape, space=pltpu.VMEM):
    return pl.BlockSpec(shape, lambda i: (0,) * len(shape), memory_space=space)


def interior(tokens, ids, rel_index, bias_table, weights):
    count = SIDE // WIN - 1
    last = count - 1
    return pl.pallas_call(
        interior_kernel,
        grid=(count + 1,),
        out_shape=jax.ShapeDtypeStruct((OUT, OUT, 2 * C), BF16),
        in_specs=[
            pl.BlockSpec(
                (pl.Element(WIN), pl.Element(SIDE), pl.Element(C)),
                lambda i: (WIN * jnp.minimum(i, last) + 4, 0, 0),
            ),
            pl.BlockSpec(
                (pl.Element(WIN), pl.Element(SIDE), pl.Element(C)),
                lambda i: (WIN * jnp.maximum(i - 1, 0) + 4, 0, 0),
            ),
            whole((STRIPS, SIDE), pltpu.SMEM),
            whole(rel_index.shape),
            whole(bias_table.shape),
        ]
        + [whole(a.shape) for a in weights],
        out_specs=pl.BlockSpec(
            (pl.Element(4), pl.Element(OUT), pl.Element(2 * C)), lambda i: (4 * jnp.maximum(i - 1, 0) + 2, 0, 0)
        ),
        scratch_shapes=[
            pltpu.VMEM((VARIANTS, SPOTS, HEADS * SPOTS), F32),
            pltpu.VMEM((C, C), BF16),
            pltpu.VMEM((C, MLP), BF16),
            pltpu.VMEM((256, 128), F32),
            pltpu.VMEM((pl.cdiv(count, GROUP), C, SPOTS * GROUP), BF16),
            pltpu.VMEM((WIN, SIDE, C), F32),
        ],
        compiler_params=pltpu.CompilerParams(vmem_limit_bytes=56 * 1024 * 1024),
    )(tokens, tokens, ids, rel_index, bias_table, *weights)


def edge_specs():
    return [
        pl.BlockSpec((4, SIDE, C), lambda i: (0, 0, 0)),
        pl.BlockSpec((4, SIDE, C), lambda i: (SIDE // 4 - 1, 0, 0)),
        pl.BlockSpec((SIDE, 8, C), lambda i: (0, 0, 0)),
        pl.BlockSpec((SIDE, 8, C), lambda i: (0, SIDE // 8 - 1, 0)),
    ]


def pack_kernel(top_ref, bottom_ref, left_ref, right_ref, regions_ref, ids_ref, *refs):
    messages, col_scr = refs[:8], refs[8]
    ids = regions_ref[pl.ds(0, STRIPS, stride=16), :]
    ids_ref[...] = ids
    coded = jnp.concatenate([ids, ids], axis=0).astype(F32).astype(BF16)
    line = 4 * SIDE
    for out, source in zip(messages[:2], (top_ref, bottom_ref)):
        for y in range(4):
            out[pl.ds(SIDE * y, SIDE), :] = source[y].astype(BF16)
    for out, source, at in zip(messages[2:4], (left_ref, right_ref), (0, 4)):
        for r in range(SIDE):
            col_scr[pl.ds(4 * r, 4), :] = source[r, pl.ds(at, 4), :]
        out[pl.ds(0, line), :] = col_scr[...].astype(BF16)
    for out in messages[:4]:
        out[pl.ds(line, IDROWS), :] = coded
    corners = ((top_ref, 0), (top_ref, SIDE - 4), (bottom_ref, 0), (bottom_ref, SIDE - 4))
    for out, (source, at) in zip(messages[4:], corners):
        for y in range(4):
            col_scr[pl.ds(4 * y, 4), :] = source[y, pl.ds(at, 4), :]
        out[pl.ds(0, 16), :] = col_scr[pl.ds(0, 16), :].astype(BF16)
        out[pl.ds(16, IDROWS), :] = coded


def pack(tokens, regions):
    line = jax.ShapeDtypeStruct((4 * SIDE + IDROWS, C), BF16)
    corner = jax.ShapeDtypeStruct((16 + IDROWS, C), BF16)
    shapes = [jax.ShapeDtypeStruct((STRIPS, SIDE), jnp.int32)] + [line] * 4 + [corner] * 4
    return pl.pallas_call(
        pack_kernel,
        grid=(1,),
        out_shape=shapes,
        in_specs=edge_specs() + [whole((SIDE, SIDE))],
        out_specs=[whole(a.shape) for a in shapes],
        scratch_shapes=[pltpu.VMEM((4 * SIDE, C), F32)],
    )(tokens, tokens, tokens, tokens, regions)


def exchange(messages):
    rows, cols = lax.axis_size("row"), lax.axis_size("col")

    def moved(value, down, along):
        if along == 0:
            return lax.ppermute(value, "row", [(i, (i + down) % rows) for i in range(rows)])
        if down == 0:
            return lax.ppermute(value, "col", [(i, (i + along) % cols) for i in range(cols)])
        pairs = [
            (r * cols + c, (r + down) % rows * cols + (c + along) % cols) for r in range(rows) for c in range(cols)
        ]
        return lax.ppermute(value, ("row", "col"), pairs)

    top, bottom, left, right, top_left, top_right, low_left, low_right = messages
    return (
        moved(bottom, 1, 0),
        moved(top, -1, 0),
        moved(right, 0, 1),
        moved(left, 0, -1),
        moved(low_right, 1, 1),
        moved(low_left, 1, -1),
        moved(top_right, -1, 1),
        moved(top_left, -1, -1),
    )


def gather_border(edges, got, x_scr, msg_scr):
    top, bottom, left, right = edges
    line = 4 * SIDE
    for n in range(4):
        msg_scr[pl.ds(line * n, line), :] = got[n][pl.ds(0, line), :].astype(F32)
    for n in range(4):
        msg_scr[pl.ds(4 * line + 16 * n, 16), :] = got[4 + n][pl.ds(0, 16), :].astype(F32)

    def row_of(n):
        return lambda y, at, size: msg_scr[pl.ds(line * n + SIDE * y + at, size), :]

    def col_of(n):
        return lambda r, at, size: msg_scr[pl.ds(line * n + 4 * r + at, size), :]

    def corner_of(n):
        return lambda y, at, size: msg_scr[pl.ds(4 * line + 16 * n + 4 * y + at, size), :]

    def own(ref):
        return lambda y, at, size: ref[y, pl.ds(at, size), :]

    above, below, from_left, from_right = row_of(0), row_of(1), col_of(2), col_of(3)
    for t in range(16):
        for y in range(8):
            spot = WIN * y
            side, at = (above, y) if y < 4 else (own(top), y - 4)
            if t == 0:
                edge = corner_of(0)(y, 0, 4) if y < 4 else from_left(y - 4, 0, 4)
                x_scr[0, t, pl.ds(spot, 4), :] = edge
                x_scr[0, t, pl.ds(spot + 4, 4), :] = side(at, 0, 4)
            else:
                x_scr[0, t, pl.ds(spot, 8), :] = side(at, 8 * t - 4, 8)
            side, at = (own(bottom), y) if y < 4 else (below, y - 4)
            if t == 15:
                edge = from_right(124 + y, 0, 4) if y < 4 else corner_of(3)(y - 4, 0, 4)
                x_scr[2, t, pl.ds(spot, 4), :] = side(at, 124, 4)
                x_scr[2, t, pl.ds(spot + 4, 4), :] = edge
            else:
                x_scr[2, t, pl.ds(spot, 8), :] = side(at, 8 * t + 4, 8)
            r = 8 * t - 4 + y
            x_scr[1, t, pl.ds(spot, 4), :] = above(y, 124, 4) if r < 0 else own(right)(r, 4, 4)
            x_scr[1, t, pl.ds(spot + 4, 4), :] = corner_of(1)(y, 0, 4) if r < 0 else from_right(r, 0, 4)
            r = 8 * t + 4 + y
            x_scr[3, t, pl.ds(spot, 4), :] = corner_of(2)(r - SIDE, 0, 4) if r >= SIDE else from_left(r, 0, 4)
            x_scr[3, t, pl.ds(spot + 4, 4), :] = below(r - SIDE, 0, 4) if r >= SIDE else own(left)(r, 0, 4)


def border_patterns(id_at, var_smem):
    for t in range(16):
        before = ((t + 1) // 2 - 1, t // 2)
        after = (t // 2, (t + 1) // 2)
        pairs = (((-1, 0), before), (before, (7, 8)), ((7, 8), after), (after, (-1, 0)))
        for s, (rs, cs) in enumerate(pairs):
            var_smem[s, t] = pattern(id_at(rs[0], cs[0]), id_at(rs[0], cs[1]), id_at(rs[1], cs[0]), id_at(rs[1], cs[1]))


def border_kernel(*refs):
    edges, own_ids, got = refs[:4], refs[4], refs[5:13]
    rel_ref, table_ref = refs[13:15]
    w = dict(zip(NAMES, refs[15:23]))
    inner_ref, out_ref = refs[23:25]
    (bias_scr, wvt_scr, wup_scr, pad_scr, att_scr, blk_scr, x_scr, msg_scr, idv_scr, ids_smem, var_smem, row_scr,
     col_scr, row_out, col_out, sem_ids, sem_in, sem_out) = refs[25:]
    step = pl.program_id(0)
    count = 16
    col_in = [
        pltpu.make_async_copy(inner_ref.at[:, pl.ds(at, 16), :], col_out.at[n], sem_in.at[n])
        for n, at in enumerate((0, OUT - 16))
    ]

    @pl.when(step == 0)
    def _():
        for copy in col_in:
            copy.start()
        for n in range(8):
            first = 4 * SIDE if n < 4 else 16
            idv_scr[pl.ds(STRIPS * n, STRIPS), :] = (
                got[n][pl.ds(first, IDROWS), :].astype(F32)[:STRIPS].astype(jnp.int32)
            )
        ids_copy = pltpu.make_async_copy(idv_scr, ids_smem, sem_ids)
        ids_copy.start()
        gather_border(edges, got, x_scr, msg_scr)
        prepare(rel_ref, table_ref, w["w_qkv"], w["w_up"], bias_scr, wvt_scr, wup_scr, pad_scr)
        ids_copy.wait()
        places = {(-1, 0): 0, (1, 0): 1, (0, -1): 2, (0, 1): 3, (-1, -1): 4, (-1, 1): 5, (1, -1): 6, (1, 1): 7}

        def id_at(m, n):
            where = (-1 if m < 0 else int(m >= STRIPS), -1 if n < 0 else int(n >= STRIPS))
            m, n = m % STRIPS, n % STRIPS
            if where == (0, 0):
                return own_ids[m, 16 * n]
            return ids_smem[STRIPS * places[where] + m, 16 * n]

        border_patterns(id_at, var_smem)

    groups = [list(range(at, at + GROUP)) for at in range(0, count, GROUP)]

    def store_att(g):
        def store(i, value):
            att_scr[g, :, pl.ds(SPOTS * i, SPOTS)] = value

        return store

    def store_block(t):
        def store(value):
            blk_scr[pl.ds(SPOTS * t, SPOTS), :] = value

        return store

    def fronts():
        return [
            (
                FRONT_EVERY * g,
                FRONT_GAP,
                front(
                    [lambda t=t: x_scr[step, t] for t in ts],
                    store_att(g),
                    [var_smem[step, t] for t in ts],
                    w,
                    bias_scr,
                    wvt_scr,
                ),
            )
            for g, ts in enumerate(groups)
        ]

    def backs():
        return [
            (
                BACK_EVERY * g,
                BACK_GAP,
                back(
                    [lambda t=t: x_scr[step - 1, t] for t in ts],
                    lambda g=g: att_scr[g],
                    [store_block(t) for t in ts],
                    w,
                    wup_scr,
                ),
            )
            for g, ts in enumerate(groups)
        ]

    @pl.when(step == 0)
    def _():
        drive(fronts())

    @pl.when((step > 0) & (step < 4))
    def _():
        drive(backs() + fronts())

    @pl.when(step == 4)
    def _():
        drive(backs())

    def spread(scr, at, first, value):
        for half in range(2):
            scr[2 * at + half, pl.ds(first, count, stride=4), :] = value[:, C * half : C * (half + 1)]

    def both(scr, at, rows):
        return jnp.concatenate([scr[2 * at + half, rows, :] for half in range(2)], axis=1)

    @pl.when(step > 0)
    def _():
        results = {}
        for a in range(4):
            joined = []
            for dx in range(2):
                for dy in range(2):
                    joined.append(
                        jnp.concatenate(
                            [
                                blk_scr[pl.ds((2 * a + dy) * WIN + 2 * b + dx, count, stride=SPOTS), :]
                                for b in range(4)
                            ],
                            axis=0,
                        )
                    )
            normed = layer_norm(jnp.concatenate(joined, axis=1), w["gm"][...]).astype(BF16)
            merged = jnp.dot(normed, w["w_merge"][...], preferred_element_type=F32)
            for b in range(4):
                results[a, b] = merged[count * b : count * (b + 1)]

        @pl.when(step == 1)
        def _():
            for a in (2, 3):
                for b in range(4):
                    spread(row_scr, a - 2, 8 + b - 2, results[a, b])

        @pl.when(step == 2)
        def _():
            for b in (0, 1):
                for a in range(4):
                    spread(col_scr, 2 + b, 8 + a - 2, results[a, b])

        @pl.when(step == 3)
        def _():
            for a in (0, 1):
                for b in range(4):
                    spread(row_scr, 2 + a, 8 + b + 2, results[a, b])

        @pl.when(step == 4)
        def _():
            for b in (2, 3):
                for a in range(4):
                    spread(col_scr, b - 2, 8 + a + 2, results[a, b])

    @pl.when(step == 4)
    def _():
        for c in range(2):
            for a in range(2):
                for h in range(2):
                    row_scr[2 * a + h, pl.ds(8 + OUT - 2 + c, 1), :] = col_scr[2 * (2 + c) + h, pl.ds(8 + a, 1), :]
                    row_scr[2 * (2 + a) + h, pl.ds(8 + c, 1), :] = col_scr[2 * c + h, pl.ds(8 + OUT - 2 + a, 1), :]
        for a in range(4):
            row_out[a] = both(row_scr, a, pl.ds(8, OUT)).astype(BF16)
        for copy in col_in:
            copy.wait()
        place = lax.broadcasted_iota(jnp.int32, (16, 2 * C), 0)
        for side, first in ((0, 0), (1, 14)):
            for r in range(2, OUT - 2):
                old = col_out[side, r].astype(F32)
                for c in range(2):
                    old = jnp.where(place == first + c, both(col_scr, 2 * side + c, pl.ds(8 + r, 1)), old)
                col_out[side, r] = old.astype(BF16)
        inside = pl.ds(2, OUT - 4)
        copies = [
            pltpu.make_async_copy(
                col_out.at[n, inside], out_ref.at[inside, pl.ds(at, 16), :], sem_out.at[n]
            )
            for n, at in enumerate((0, OUT - 16))
        ]
        copies += [
            pltpu.make_async_copy(row_out.at[pl.ds(2 * n, 2)], out_ref.at[pl.ds(at, 2)], sem_out.at[2 + n])
            for n, at in enumerate((0, OUT - 2))
        ]
        for copy in copies:
            copy.start()
        for copy in copies:
            copy.wait()


def border(tokens, ids, got, rel_index, bias_table, weights, inner):
    line = 4 * SIDE
    return pl.pallas_call(
        border_kernel,
        grid=(5,),
        out_shape=jax.ShapeDtypeStruct((OUT, OUT, 2 * C), BF16),
        in_specs=edge_specs()
        + [whole((STRIPS, SIDE), pltpu.SMEM)]
        + [whole(a.shape) for a in got]
        + [whole(rel_index.shape), whole(bias_table.shape)]
        + [whole(a.shape) for a in weights]
        + [pl.BlockSpec(memory_space=pl.ANY)],
        out_specs=pl.BlockSpec(memory_space=pl.ANY),
        input_output_aliases={15 + len(weights): 0},
        scratch_shapes=[
            pltpu.VMEM((VARIANTS, SPOTS, HEADS * SPOTS), F32),
            pltpu.VMEM((C, C), BF16),
            pltpu.VMEM((C, MLP), BF16),
            pltpu.VMEM((256, 128), F32),
            pltpu.VMEM((16 // GROUP, C, SPOTS * GROUP), BF16),
            pltpu.VMEM((16 * SPOTS, C), F32),
            pltpu.VMEM((4, 16, SPOTS, C), F32),
            pltpu.VMEM((4 * line + 64, C), F32),
            pltpu.VMEM((8 * STRIPS, SIDE), jnp.int32),
            pltpu.SMEM((8 * STRIPS, SIDE), jnp.int32),
            pltpu.SMEM((4, 16), jnp.int32),
            pltpu.VMEM((8, OUT + 16, C), F32),
            pltpu.VMEM((8, OUT + 16, C), F32),
            pltpu.VMEM((4, OUT, 2 * C), BF16),
            pltpu.VMEM((2, OUT, 16, 2 * C), BF16),
            pltpu.SemaphoreType.DMA,
            pltpu.SemaphoreType.DMA((2,)),
            pltpu.SemaphoreType.DMA((4,)),
        ],
        compiler_params=pltpu.CompilerParams(vmem_limit_bytes=56 * 1024 * 1024),
    )(tokens, tokens, tokens, tokens, ids, *got, rel_index, bias_table, *weights, inner)


def on_device(
    tokens, regions, rel_index, bias_table, norm1_gain, w_qkv, w_proj, norm2_gain, w_up, w_down, merge_gain, w_merge
):
    weights = (
        norm1_gain.reshape(1, C), w_qkv, w_proj, norm2_gain.reshape(1, C), w_up, w_down,
        merge_gain.reshape(1, 4 * C), w_merge,
    )
    ids, *messages = pack(tokens, regions)
    got = exchange(messages)
    inner = interior(tokens, ids, rel_index, bias_table, weights)
    return border(tokens, ids, got, rel_index, bias_table, weights, inner)


def solution(mesh):
    return jax.shard_map(
        on_device,
        mesh=mesh,
        in_specs=(P("row", "col", None), P("row", "col")) + (P(),) * 10,
        out_specs=P("row", "col", None),
        check_vma=False,
    )
```

time: 390 us -> 112 us (0.29); the launches traced: 385 us -> 111 us
  local copies, waits for them, and re-layouts: 171 us -> 2.16 us
  matrix products: 111 us -> 0 us
  Pallas kernels: 0 us -> 73.9 us
  other arithmetic: 69.2 us -> 0 us
    slice x43 -> x0, local copies, waits for them, and re-layouts: 143 us -> none  [the longest x1 33.4 us: merge_patches(): block[0::2, 1::2]]
    pallas_call x0 -> x3, Pallas kernels: none -> 73.9 us  [the longest x1 51.2 us: interior(): pl.pallas_call(interior_kernel, grid=(count + 1,), out_shape=jax.ShapeDty...]
    dot_general x66 -> x0, matrix products: 70.3 us -> none  [the longest x16 33.7 us: attend_row(): jnp.einsum('whqk,wkc->whqc', probs, values, preferred_element_type=jnp.fl...]
    reduce_sum x53 -> x0, other arithmetic: 42.8 us -> none  [the longest x20 27.2 us: layer_norm(): mean = jnp.mean(values, axis=-1, keepdims=True)]
    sub x16 -> x0, matrix products: 40.3 us -> none  [attend_row(): expo = jnp.exp(scores - top)]
    dynamic_update_slice x16 -> x0, local copies, waits for them, and re-layouts: 13.7 us -> none  [on_device(): block_out = from_windows(lax.map(run_block, (windows, window_ids)), side)]
    concatenate x6 -> x0, other arithmetic: 11.7 us -> none  [the longest x1 7.38 us: on_device(): jnp.concatenate([jnp.concatenate([tokens[SHIFT:, SHIFT:], right[:side - S...]
    convert_element_type x33 -> x0, other arithmetic: 5.64 us -> none  [the longest x16 5.52 us: attend_row(): normed = layer_norm(flat, norm1_gain).astype(jnp.bfloat16)]
  transfers between devices with their start and end apart: 6 -> 8, of which waited for: 3 -> 3; matrix products, arithmetic and copies ran while one was open for 4% -> 1% of each run, Pallas kernels for 0% -> 46%
where the time goes in v1:
time: 112 us; the launch traced here: 111 us
  Pallas kernels  73.9 us (66%)
  waiting for transfers between devices  22.2 us (20%)
  starting transfers between devices  12.3 us (11%)
  local copies, waits for them, and re-layouts  2.16 us (2%)
    pallas_call x1, Pallas kernels, interior(): pl.pallas_call(interior_kernel, grid=(count + 1,), out_shape=jax.ShapeDty...  51.2 us
    ppermute x4, waiting for transfers between devices, moved(): return lax.ppermute(value, ('row', 'col'), pairs)  22.2 us
    pallas_call x1, Pallas kernels, border(): pl.pallas_call(border_kernel, grid=(5,), out_shape=jax.ShapeDtypeStruct((...  20.5 us
    ppermute x2, starting transfers between devices, moved(): lax.ppermute(value, 'col', [(i, (i + along) % cols) for i in range(cols)])  6.75 us
    ppermute x2, starting transfers between devices, moved(): lax.ppermute(value, 'row', [(i, (i + down) % rows) for i in range(rows)])  3.85 us
  transfers between devices with their start and end apart: 8, of which 3 were waited for; matrix products, arithmetic and copies ran while one was open for 1% of the time, Pallas kernels for 46%

profile of v1, /device:TPU:0, one launch (start us, length us, event | category | flops | bytes accessed | tf_op | source)
XLA Modules:
  0.0 110.8 jit_solution(2744521340530623439)
XLA Ops:
  0.0 2.2 %shard_map.118 = (s32[8,128]{1,0:T(8,128)}, bf16[528,128]{1,0:T(8,128)(2,1)}, bf16[528,128]{1,0:T(8,128)(2,1)}, bf16[528,128]{1,0:T(8,128)(2,1)}, bf16[528,128]{...) custom-call(f32[128,128,128]{2,1,0:T(8,128)} %refs_3_.1, ...), custom_call_target="tpu_custom_call" | custom-call | tf_op jit(solution)/shard_map/pallas_call | solution.py:354
  2.2 0.0 collective-permute-start
  2.2 3.9 %collective-permute-start.1 = (bf16[528,128]{1,0:T(8,128)(2,1)}, bf16[528,128]{1,0:T(8,128)(2,1)S(1)}, u32[]{:S(2)}, u32[]{:S(2)}) collective-permute-start(bf16[528,128]{1,0:T(8,128)(2,1)} %get-tuple-element.16), channel_id=1, source_target_pairs={{0,240},{16,0},{32,16},{48,32},{64,48},{80,64},{96,80},{112,96},{1... | collective-permute-start | bytes 405512 | tf_op jit(solution)/shard_map/ppermute | solution.py:369
  6.1 1.5 %collective-permute-start.2 = (bf16[528,128]{1,0:T(8,128)(2,1)}, bf16[528,128]{1,0:T(8,128)(2,1)S(1)}, u32[]{:S(2)}, u32[]{:S(2)}) collective-permute-start(bf16[528,128]{1,0:T(8,128)(2,1)} %get-tuple-element.17), channel_id=1, source_target_pairs={{0,1},{1,2},{2,3},{3,4},{4,5},{5,6},{6,7},{7,8},{8,9},{9,10},{10,1... | collective-permute-start | bytes 405512 | tf_op jit(solution)/shard_map/ppermute | solution.py:371
  7.5 5.3 %collective-permute-start.3 = (bf16[528,128]{1,0:T(8,128)(2,1)}, bf16[528,128]{1,0:T(8,128)(2,1)S(1)}, u32[]{:S(2)}, u32[]{:S(2)}) collective-permute-start(bf16[528,128]{1,0:T(8,128)(2,1)} %get-tuple-element.18), channel_id=1, source_target_pairs={{0,15},{1,0},{2,1},{3,2},{4,3},{5,4},{6,5},{7,6},{8,7},{9,8},{10,9... | collective-permute-start | bytes 405512 | tf_op jit(solution)/shard_map/ppermute | solution.py:371
  12.8 0.0 collective-permute-start.4
  12.8 8.7 %collective-permute-done.4.refs_9_ = bf16[32,128]{1,0:T(8,128)(2,1)S(1)} collective-permute-done((bf16[32,128]{1,0:T(8,128)(2,1)}, bf16[32,128]{1,0:T(8,128)(2,1)S(1)}, u32[]{:S(2)}, u32[]{:S(2)}) %collective-permute-start.4) | collective-permute-done | bytes 8224 | tf_op jit(solution)/shard_map/ppermute | solution.py:375
  21.5 0.0 collective-permute-start.5
  21.6 6.6 %collective-permute-done.5.refs_10_ = bf16[32,128]{1,0:T(8,128)(2,1)S(1)} collective-permute-done((bf16[32,128]{1,0:T(8,128)(2,1)}, bf16[32,128]{1,0:T(8,128)(2,1)S(1)}, u32[]{:S(2)}, u32[]{:S(2)}) %collective-permute-start.5) | collective-permute-done | bytes 8224 | tf_op jit(solution)/shard_map/ppermute | solution.py:375
  28.2 0.0 collective-permute-start.6
  28.2 6.9 %collective-permute-done.6.refs_11_ = bf16[32,128]{1,0:T(8,128)(2,1)S(1)} collective-permute-done((bf16[32,128]{1,0:T(8,128)(2,1)}, bf16[32,128]{1,0:T(8,128)(2,1)S(1)}, u32[]{:S(2)}, u32[]{:S(2)}) %collective-permute-start.6) | collective-permute-done | bytes 8224 | tf_op jit(solution)/shard_map/ppermute | solution.py:375
  35.1 1.6 %collective-permute-start.7 = (bf16[32,128]{1,0:T(8,128)(2,1)}, bf16[32,128]{1,0:T(8,128)(2,1)S(1)}, u32[]{:S(2)}, u32[]{:S(2)}) collective-permute-start(bf16[32,128]{1,0:T(8,128)(2,1)} %get-tuple-element.22), channel_id=1, source_target_pairs={{0,255},{1,240},{2,241},{3,242},{4,243},{5,244},{6,245},{7,246},{8... | collective-permute-start | bytes 24584 | tf_op jit(solution)/shard_map/ppermute | solution.py:375
  36.7 0.0 copy-done.8
  36.7 0.8 copy.15.table_ref.refs_14_
  37.4 51.2 %shard_map.119.refs_23_ = bf16[64,64,256]{2,1,0:T(8,128)(2,1)} custom-call(f32[128,128,128]{2,1,0:T(8,128)} %refs_3_.1, f32[128,128,128]{2,1,0:T(8,128)} %refs_3_.1, s32[8,128]{1,0:T(8,128)} %get-tuple-element.14.ids_ref.refs_4_, s32[64,64]{1,0:T(8,128)} %refs_13_.1, f32[225,4]{1,0:T(8,128)} %copy.15.table_ref.refs_14_, f32[1,128]{1,0:T(1,128)} %bitcast.5, ...), custom_call_target="tpu_custom_call" | custom-call | tf_op jit(solution)/shard_map/pallas_call | solution.py:285
  88.6 0.0 copy-done.4
  88.6 0.0 copy-done.5
  88.6 0.0 copy-done.6
  88.6 0.0 collective-permute-done.7.refs_12_
  88.7 0.0 copy-start.7
  88.7 0.0 collective-permute-done.refs_5_
  88.7 0.0 copy-start
  88.7 0.0 collective-permute-done.1.refs_6_
  88.7 0.0 copy-start.1
  88.7 0.0 collective-permute-done.2.refs_7_
  88.7 0.0 collective-permute-done.3.refs_8_
  88.7 0.5 copy-done.7
  89.3 0.1 copy-done
  89.3 0.1 copy-done.1
  89.4 0.1 copy-done.2
  89.4 0.7 copy-done.3
  90.1 20.5 %shard_map.120 = bf16[64,64,256]{2,1,0:T(8,128)(2,1)} custom-call(f32[128,128,128]{2,1,0:T(8,128)} %refs_3_.1, f32[128,128,128]{2,1,0:T(8,128)} %refs_3_.1, f32[128,128,128]{2,1,0:T(8,128)} %refs_3_.1, f32[128,128,128]{2,1,0:T(8,128)} %refs_3_.1, s32[8,128]{1,0:T(8,128)} %get-tuple-element.14.ids_ref.refs_4_, ...), custom_call_target="tpu_custom_call", output_to_operand_aliasing={{}: (23, {})} | custom-call | tf_op jit(solution)/shard_map/pallas_call | solution.py:632
  (6 shorter events, 0.0 us)
Async XLA Ops:
  0.0 36.7 %copy-start.8 = (f32[225,4]{0,1:T(4,128)S(1)}, f32[225,4]{0,1:T(4,128)}, u32[]{:S(2)}) copy-start(f32[225,4]{0,1:T(4,128)} %param.15) | copy-start | bytes 10804
  2.2 86.5 %collective-permute-start = (bf16[528,128]{1,0:T(8,128)(2,1)}, bf16[528,128]{1,0:T(8,128)(2,1)S(1)}, u32[]{:S(2)}, u32[]{:S(2)}) collective-permute-start(bf16[528,128]{1,0:T(8,128)(2,1)} %get-tuple-element.15), channel_id=1, source_target_pairs={{0,16},{16,32},{32,48},{48,64},{64,80},{80,96},{96,112},{112,128},... | collective-permute-start | bytes 405512 | tf_op jit(solution)/shard_map/ppermute | solution.py:369
  2.2 86.5 %collective-permute-start.1 = (bf16[528,128]{1,0:T(8,128)(2,1)}, bf16[528,128]{1,0:T(8,128)(2,1)S(1)}, u32[]{:S(2)}, u32[]{:S(2)}) collective-permute-start(bf16[528,128]{1,0:T(8,128)(2,1)} %get-tuple-element.16), channel_id=1, source_target_pairs={{0,240},{16,0},{32,16},{48,32},{64,48},{80,64},{96,80},{112,96},{1... | collective-permute-start | bytes 405512 | tf_op jit(solution)/shard_map/ppermute | solution.py:369
  6.1 82.6 %collective-permute-start.2 = (bf16[528,128]{1,0:T(8,128)(2,1)}, bf16[528,128]{1,0:T(8,128)(2,1)S(1)}, u32[]{:S(2)}, u32[]{:S(2)}) collective-permute-start(bf16[528,128]{1,0:T(8,128)(2,1)} %get-tuple-element.17), channel_id=1, source_target_pairs={{0,1},{1,2},{2,3},{3,4},{4,5},{5,6},{6,7},{7,8},{8,9},{9,10},{10,1... | collective-permute-start | bytes 405512 | tf_op jit(solution)/shard_map/ppermute | solution.py:371
  7.5 81.2 %collective-permute-start.3 = (bf16[528,128]{1,0:T(8,128)(2,1)}, bf16[528,128]{1,0:T(8,128)(2,1)S(1)}, u32[]{:S(2)}, u32[]{:S(2)}) collective-permute-start(bf16[528,128]{1,0:T(8,128)(2,1)} %get-tuple-element.18), channel_id=1, source_target_pairs={{0,15},{1,0},{2,1},{3,2},{4,3},{5,4},{6,5},{7,6},{8,7},{9,8},{10,9... | collective-permute-start | bytes 405512 | tf_op jit(solution)/shard_map/ppermute | solution.py:371
  12.8 8.7 %collective-permute-start.4 = (bf16[32,128]{1,0:T(8,128)(2,1)}, bf16[32,128]{1,0:T(8,128)(2,1)S(1)}, u32[]{:S(2)}, u32[]{:S(2)}) collective-permute-start(bf16[32,128]{1,0:T(8,128)(2,1)} %get-tuple-element.19), channel_id=1, source_target_pairs={{0,17},{1,18},{2,19},{3,20},{4,21},{5,22},{6,23},{7,24},{8,25},{9,... | collective-permute-start | bytes 24584 | tf_op jit(solution)/shard_map/ppermute | solution.py:375
  21.5 67.1 %copy-start.4 = (bf16[32,128]{1,0:T(8,128)(2,1)}, bf16[32,128]{1,0:T(8,128)(2,1)S(1)}, u32[]{:S(2)}) copy-start(bf16[32,128]{1,0:T(8,128)(2,1)S(1)} %collective-permute-done.4.refs_9_) | copy-start | bytes 24580
  21.5 6.6 %collective-permute-start.5 = (bf16[32,128]{1,0:T(8,128)(2,1)}, bf16[32,128]{1,0:T(8,128)(2,1)S(1)}, u32[]{:S(2)}, u32[]{:S(2)}) collective-permute-start(bf16[32,128]{1,0:T(8,128)(2,1)} %get-tuple-element.20), channel_id=1, source_target_pairs={{0,31},{1,16},{2,17},{3,18},{4,19},{5,20},{6,21},{7,22},{8,23},{9,... | collective-permute-start | bytes 24584 | tf_op jit(solution)/shard_map/ppermute | solution.py:375
  28.2 60.5 %copy-start.5 = (bf16[32,128]{1,0:T(8,128)(2,1)}, bf16[32,128]{1,0:T(8,128)(2,1)S(1)}, u32[]{:S(2)}) copy-start(bf16[32,128]{1,0:T(8,128)(2,1)S(1)} %collective-permute-done.5.refs_10_) | copy-start | bytes 24580
  28.2 6.9 %collective-permute-start.6 = (bf16[32,128]{1,0:T(8,128)(2,1)}, bf16[32,128]{1,0:T(8,128)(2,1)S(1)}, u32[]{:S(2)}, u32[]{:S(2)}) collective-permute-start(bf16[32,128]{1,0:T(8,128)(2,1)} %get-tuple-element.21), channel_id=1, source_target_pairs={{0,241},{1,242},{2,243},{3,244},{4,245},{5,246},{6,247},{7,248},{8... | collective-permute-start | bytes 24584 | tf_op jit(solution)/shard_map/ppermute | solution.py:375
  35.1 53.6 %copy-start.6 = (bf16[32,128]{1,0:T(8,128)(2,1)}, bf16[32,128]{1,0:T(8,128)(2,1)S(1)}, u32[]{:S(2)}) copy-start(bf16[32,128]{1,0:T(8,128)(2,1)S(1)} %collective-permute-done.6.refs_11_) | copy-start | bytes 24580
  35.1 53.6 %collective-permute-start.7 = (bf16[32,128]{1,0:T(8,128)(2,1)}, bf16[32,128]{1,0:T(8,128)(2,1)S(1)}, u32[]{:S(2)}, u32[]{:S(2)}) collective-permute-start(bf16[32,128]{1,0:T(8,128)(2,1)} %get-tuple-element.22), channel_id=1, source_target_pairs={{0,255},{1,240},{2,241},{3,242},{4,243},{5,244},{6,245},{7,246},{8... | collective-permute-start | bytes 24584 | tf_op jit(solution)/shard_map/ppermute | solution.py:375
  88.7 0.6 copy-start.7
  88.7 0.7 copy-start
  88.7 0.7 copy-start.1
  88.7 0.7 copy-start.2
  89.4 0.7 copy-start.3

commit v2 on v1

--- a/solution.py
+++ b/solution.py
@@ -17,6 +17,7 @@
 OUT = SIDE // 2
 STRIPS = SIDE // 16
 IDROWS = 16
+EARLY = 3
 LOG2E = 1.4426950408889634
 QSCALE = HD ** (-0.5) * LOG2E
 VARIANTS = 24
@@ -189,9 +190,9 @@
 MERGE_EVERY, MERGE_GAP, MERGE_AT = 1.0, 1.0, 50
 
 
-def interior_kernel(x_ref, old_ref, ids_ref, rel_ref, table_ref, *refs):
+def interior_kernel(first, total, x_ref, old_ref, ids_ref, rel_ref, table_ref, *refs):
     w = dict(zip(NAMES, refs[:8]))
-    out_ref, bias_scr, wvt_scr, wup_scr, pad_scr, att_scr, blk_scr = refs[8:]
+    out_ref, bias_scr, wvt_scr, wup_scr, pad_scr, att_scr, blk_scr = refs[-7:]
     step = pl.program_id(0)
     count = SIDE // WIN - 1
 
@@ -200,7 +201,8 @@
         prepare(rel_ref, table_ref, w["w_qkv"], w["w_up"], bias_scr, wvt_scr, wup_scr, pad_scr)
         blk_scr[...] = jnp.zeros_like(blk_scr)
 
-    upper, lower = step // 2, (step + 1) // 2
+    upper = jnp.minimum(first + step, count - 1) // 2
+    lower = jnp.minimum(first + step + 1, count) // 2
 
     def loader(ref, j):
         return lambda: jnp.concatenate([ref[y, pl.ds(WIN * j + 4, WIN), :] for y in range(WIN)], axis=0)
@@ -266,11 +268,11 @@
     def _():
         drive(fronts())
 
-    @pl.when((step > 0) & (step < count))
+    @pl.when((step > 0) & (step < total))
     def _():
         drive(backs() + fronts() + merges())
 
-    @pl.when(step == count)
+    @pl.when(step == total)
     def _():
         drive(backs() + merges())
 
@@ -279,157 +281,157 @@
     return pl.BlockSpec(shape, lambda i: (0,) * len(shape), memory_space=space)
 
 
-def interior(tokens, ids, rel_index, bias_table, weights):
-    count = SIDE // WIN - 1
-    last = count - 1
+def interior(tokens, ids, rel_index, bias_table, weights, first, total, before=None, after=None):
+    groups = pl.cdiv(SIDE // WIN - 1, GROUP)
+    strip = (pl.Element(WIN), pl.Element(SIDE), pl.Element(C))
+    extra = () if before is None else (before, after)
+    args = (tokens, tokens, ids, rel_index, bias_table, *weights, *extra)
     return pl.pallas_call(
-        interior_kernel,
-        grid=(count + 1,),
+        functools.partial(interior_kernel, first, total),
+        grid=(total + 1,),
         out_shape=jax.ShapeDtypeStruct((OUT, OUT, 2 * C), BF16),
         in_specs=[
-            pl.BlockSpec(
-                (pl.Element(WIN), pl.Element(SIDE), pl.Element(C)),
-                lambda i: (WIN * jnp.minimum(i, last) + 4, 0, 0),
-            ),
-            pl.BlockSpec(
-                (pl.Element(WIN), pl.Element(SIDE), pl.Element(C)),
-                lambda i: (WIN * jnp.maximum(i - 1, 0) + 4, 0, 0),
-            ),
+            pl.BlockSpec(strip, lambda i: (WIN * (first + jnp.minimum(i, total - 1)) + 4, 0, 0)),
+            pl.BlockSpec(strip, lambda i: (WIN * (first + jnp.maximum(i - 1, 0)) + 4, 0, 0)),
             whole((STRIPS, SIDE), pltpu.SMEM),
             whole(rel_index.shape),
             whole(bias_table.shape),
         ]
-        + [whole(a.shape) for a in weights],
+        + [whole(a.shape) for a in weights]
+        + [pl.BlockSpec(memory_space=pl.ANY) for _ in extra],
         out_specs=pl.BlockSpec(
-            (pl.Element(4), pl.Element(OUT), pl.Element(2 * C)), lambda i: (4 * jnp.maximum(i - 1, 0) + 2, 0, 0)
+            (pl.Element(4), pl.Element(OUT), pl.Element(2 * C)),
+            lambda i: (4 * (first + jnp.maximum(i - 1, 0)) + 2, 0, 0),
         ),
+        input_output_aliases={} if before is None else {len(args) - 2: 0},
         scratch_shapes=[
             pltpu.VMEM((VARIANTS, SPOTS, HEADS * SPOTS), F32),
             pltpu.VMEM((C, C), BF16),
             pltpu.VMEM((C, MLP), BF16),
             pltpu.VMEM((256, 128), F32),
-            pltpu.VMEM((pl.cdiv(count, GROUP), C, SPOTS * GROUP), BF16),
+            pltpu.VMEM((groups, C, SPOTS * GROUP), BF16),
             pltpu.VMEM((WIN, SIDE, C), F32),
         ],
         compiler_params=pltpu.CompilerParams(vmem_limit_bytes=56 * 1024 * 1024),
-    )(tokens, tokens, ids, rel_index, bias_table, *weights)
-
-
-def edge_specs():
+    )(*args)
+
+
+LINE = 4 * SIDE
+BAND = 4 * (SIDE + 8)
+
+
+def row_specs():
     return [
         pl.BlockSpec((4, SIDE, C), lambda i: (0, 0, 0)),
         pl.BlockSpec((4, SIDE, C), lambda i: (SIDE // 4 - 1, 0, 0)),
+    ]
+
+
+def col_specs():
+    return [
         pl.BlockSpec((SIDE, 8, C), lambda i: (0, 0, 0)),
         pl.BlockSpec((SIDE, 8, C), lambda i: (0, SIDE // 8 - 1, 0)),
     ]
 
 
-def pack_kernel(top_ref, bottom_ref, left_ref, right_ref, regions_ref, ids_ref, *refs):
-    messages, col_scr = refs[:8], refs[8]
+def pack_rows_kernel(top_ref, bottom_ref, regions_ref, ids_ref, *messages):
     ids = regions_ref[pl.ds(0, STRIPS, stride=16), :]
     ids_ref[...] = ids
     coded = jnp.concatenate([ids, ids], axis=0).astype(F32).astype(BF16)
-    line = 4 * SIDE
-    for out, source in zip(messages[:2], (top_ref, bottom_ref)):
+    for out, source in zip(messages, (top_ref, bottom_ref)):
         for y in range(4):
             out[pl.ds(SIDE * y, SIDE), :] = source[y].astype(BF16)
-    for out, source, at in zip(messages[2:4], (left_ref, right_ref), (0, 4)):
-        for r in range(SIDE):
-            col_scr[pl.ds(4 * r, 4), :] = source[r, pl.ds(at, 4), :]
-        out[pl.ds(0, line), :] = col_scr[...].astype(BF16)
-    for out in messages[:4]:
-        out[pl.ds(line, IDROWS), :] = coded
-    corners = ((top_ref, 0), (top_ref, SIDE - 4), (bottom_ref, 0), (bottom_ref, SIDE - 4))
-    for out, (source, at) in zip(messages[4:], corners):
-        for y in range(4):
-            col_scr[pl.ds(4 * y, 4), :] = source[y, pl.ds(at, 4), :]
-        out[pl.ds(0, 16), :] = col_scr[pl.ds(0, 16), :].astype(BF16)
-        out[pl.ds(16, IDROWS), :] = coded
-
-
-def pack(tokens, regions):
-    line = jax.ShapeDtypeStruct((4 * SIDE + IDROWS, C), BF16)
-    corner = jax.ShapeDtypeStruct((16 + IDROWS, C), BF16)
-    shapes = [jax.ShapeDtypeStruct((STRIPS, SIDE), jnp.int32)] + [line] * 4 + [corner] * 4
+        out[pl.ds(LINE, IDROWS), :] = coded
+
+
+def pack_rows(tokens, regions):
+    line = jax.ShapeDtypeStruct((LINE + IDROWS, C), BF16)
+    shapes = [jax.ShapeDtypeStruct((STRIPS, SIDE), jnp.int32), line, line]
     return pl.pallas_call(
-        pack_kernel,
+        pack_rows_kernel,
         grid=(1,),
         out_shape=shapes,
-        in_specs=edge_specs() + [whole((SIDE, SIDE))],
+        in_specs=row_specs() + [whole((SIDE, SIDE))],
         out_specs=[whole(a.shape) for a in shapes],
-        scratch_shapes=[pltpu.VMEM((4 * SIDE, C), F32)],
-    )(tokens, tokens, tokens, tokens, regions)
-
-
-def exchange(messages):
-    rows, cols = lax.axis_size("row"), lax.axis_size("col")
-
-    def moved(value, down, along):
-        if along == 0:
-            return lax.ppermute(value, "row", [(i, (i + down) % rows) for i in range(rows)])
-        if down == 0:
-            return lax.ppermute(value, "col", [(i, (i + along) % cols) for i in range(cols)])
-        pairs = [
-            (r * cols + c, (r + down) % rows * cols + (c + along) % cols) for r in range(rows) for c in range(cols)
-        ]
-        return lax.ppermute(value, ("row", "col"), pairs)
-
-    top, bottom, left, right, top_left, top_right, low_left, low_right = messages
-    return (
-        moved(bottom, 1, 0),
-        moved(top, -1, 0),
-        moved(right, 0, 1),
-        moved(left, 0, -1),
-        moved(low_right, 1, 1),
-        moved(low_left, 1, -1),
-        moved(top_right, -1, 1),
-        moved(top_left, -1, -1),
-    )
+    )(tokens, tokens, regions)
+
+
+def pack_cols_kernel(left_ref, right_ref, above_ref, below_ref, ids_ref, after_ref, to_left, to_right, token_ref, band_scr, row_scr):
+    token_ref[...] = jnp.zeros_like(token_ref)
+    row_scr[0] = above_ref[pl.ds(0, LINE), :].astype(F32)
+    row_scr[1] = below_ref[pl.ds(0, LINE), :].astype(F32)
+    ids = ids_ref[...]
+    own = jnp.concatenate([ids, ids], axis=0).astype(F32).astype(BF16)
+    for out, source, at, far in ((to_left, left_ref, 0, 0), (to_right, right_ref, 4, SIDE - 4)):
+        for y in range(4):
+            band_scr[pl.ds(4 * y, 4), :] = row_scr[0, pl.ds(SIDE * y + far, 4), :]
+            band_scr[pl.ds(4 * (SIDE + 4 + y), 4), :] = row_scr[1, pl.ds(SIDE * y + far, 4), :]
+        for r in range(SIDE):
+            band_scr[pl.ds(4 * (r + 4), 4), :] = source[r, pl.ds(at, 4), :]
+        out[pl.ds(0, BAND), :] = band_scr[...].astype(BF16)
+        out[pl.ds(BAND, IDROWS), :] = above_ref[pl.ds(LINE, IDROWS), :]
+        out[pl.ds(BAND + IDROWS, IDROWS), :] = own
+        out[pl.ds(BAND + 2 * IDROWS, IDROWS), :] = below_ref[pl.ds(LINE, IDROWS), :]
+
+
+def pack_cols(tokens, above, below, ids, after):
+    band = jax.ShapeDtypeStruct((BAND + 3 * IDROWS, C), BF16)
+    token = jax.ShapeDtypeStruct((8, C), F32)
+    return pl.pallas_call(
+        pack_cols_kernel,
+        grid=(1,),
+        out_shape=[band, band, token],
+        in_specs=col_specs()
+        + [whole(above.shape), whole(below.shape), whole(ids.shape), pl.BlockSpec(memory_space=pl.ANY)],
+        out_specs=[whole(band.shape), whole(band.shape), whole(token.shape)],
+        scratch_shapes=[pltpu.VMEM((BAND, C), F32), pltpu.VMEM((2, LINE, C), F32)],
+    )(tokens, tokens, above, below, ids, after)
+
+
+def moved(value, axis, by):
+    size = lax.axis_size(axis)
+    return lax.ppermute(value, axis, [(i, (i + by) % size) for i in range(size)])
 
 
 def gather_border(edges, got, x_scr, msg_scr):
     top, bottom, left, right = edges
     line = 4 * SIDE
-    for n in range(4):
+    for n in range(2):
         msg_scr[pl.ds(line * n, line), :] = got[n][pl.ds(0, line), :].astype(F32)
-    for n in range(4):
-        msg_scr[pl.ds(4 * line + 16 * n, 16), :] = got[4 + n][pl.ds(0, 16), :].astype(F32)
+        msg_scr[pl.ds(2 * line + BAND * n, BAND), :] = got[2 + n][pl.ds(0, BAND), :].astype(F32)
 
     def row_of(n):
         return lambda y, at, size: msg_scr[pl.ds(line * n + SIDE * y + at, size), :]
 
     def col_of(n):
-        return lambda r, at, size: msg_scr[pl.ds(line * n + 4 * r + at, size), :]
-
-    def corner_of(n):
-        return lambda y, at, size: msg_scr[pl.ds(4 * line + 16 * n + 4 * y + at, size), :]
+        return lambda r, at, size: msg_scr[pl.ds(2 * line + BAND * n + 4 * (r + 4) + at, size), :]
 
     def own(ref):
         return lambda y, at, size: ref[y, pl.ds(at, size), :]
 
-    above, below, from_left, from_right = row_of(0), row_of(1), col_of(2), col_of(3)
+    above, below, from_left, from_right = row_of(0), row_of(1), col_of(0), col_of(1)
     for t in range(16):
         for y in range(8):
             spot = WIN * y
             side, at = (above, y) if y < 4 else (own(top), y - 4)
             if t == 0:
-                edge = corner_of(0)(y, 0, 4) if y < 4 else from_left(y - 4, 0, 4)
+                edge = from_left(y - 4, 0, 4)
                 x_scr[0, t, pl.ds(spot, 4), :] = edge
                 x_scr[0, t, pl.ds(spot + 4, 4), :] = side(at, 0, 4)
             else:
                 x_scr[0, t, pl.ds(spot, 8), :] = side(at, 8 * t - 4, 8)
             side, at = (own(bottom), y) if y < 4 else (below, y - 4)
             if t == 15:
-                edge = from_right(124 + y, 0, 4) if y < 4 else corner_of(3)(y - 4, 0, 4)
+                edge = from_right(124 + y, 0, 4)
                 x_scr[2, t, pl.ds(spot, 4), :] = side(at, 124, 4)
                 x_scr[2, t, pl.ds(spot + 4, 4), :] = edge
             else:
                 x_scr[2, t, pl.ds(spot, 8), :] = side(at, 8 * t + 4, 8)
             r = 8 * t - 4 + y
             x_scr[1, t, pl.ds(spot, 4), :] = above(y, 124, 4) if r < 0 else own(right)(r, 4, 4)
-            x_scr[1, t, pl.ds(spot + 4, 4), :] = corner_of(1)(y, 0, 4) if r < 0 else from_right(r, 0, 4)
+            x_scr[1, t, pl.ds(spot + 4, 4), :] = from_right(r, 0, 4)
             r = 8 * t + 4 + y
-            x_scr[3, t, pl.ds(spot, 4), :] = corner_of(2)(r - SIDE, 0, 4) if r >= SIDE else from_left(r, 0, 4)
+            x_scr[3, t, pl.ds(spot, 4), :] = from_left(r, 0, 4)
             x_scr[3, t, pl.ds(spot + 4, 4), :] = below(r - SIDE, 0, 4) if r >= SIDE else own(left)(r, 0, 4)
 
 
@@ -443,12 +445,12 @@
 
 
 def border_kernel(*refs):
-    edges, own_ids, got = refs[:4], refs[4], refs[5:13]
-    rel_ref, table_ref = refs[13:15]
-    w = dict(zip(NAMES, refs[15:23]))
-    inner_ref, out_ref = refs[23:25]
+    edges, own_ids, got = refs[:4], refs[4], refs[5:9]
+    rel_ref, table_ref = refs[9:11]
+    w = dict(zip(NAMES, refs[11:19]))
+    inner_ref, out_ref = refs[19:21]
     (bias_scr, wvt_scr, wup_scr, pad_scr, att_scr, blk_scr, x_scr, msg_scr, idv_scr, ids_smem, var_smem, row_scr,
-     col_scr, row_out, col_out, sem_ids, sem_in, sem_out) = refs[25:]
+     col_scr, row_out, col_out, sem_ids, sem_in, sem_out) = refs[21:]
     step = pl.program_id(0)
     count = 16
     col_in = [
@@ -460,17 +462,18 @@
     def _():
         for copy in col_in:
             copy.start()
-        for n in range(8):
-            first = 4 * SIDE if n < 4 else 16
+        places = [(0, LINE), (1, LINE)]
+        places += [(2 + side, BAND + IDROWS * m) for side in range(2) for m in range(3)]
+        for n, (source, first) in enumerate(places):
             idv_scr[pl.ds(STRIPS * n, STRIPS), :] = (
-                got[n][pl.ds(first, IDROWS), :].astype(F32)[:STRIPS].astype(jnp.int32)
+                got[source][pl.ds(first, IDROWS), :].astype(F32)[:STRIPS].astype(jnp.int32)
             )
         ids_copy = pltpu.make_async_copy(idv_scr, ids_smem, sem_ids)
         ids_copy.start()
         gather_border(edges, got, x_scr, msg_scr)
         prepare(rel_ref, table_ref, w["w_qkv"], w["w_up"], bias_scr, wvt_scr, wup_scr, pad_scr)
         ids_copy.wait()
-        places = {(-1, 0): 0, (1, 0): 1, (0, -1): 2, (0, 1): 3, (-1, -1): 4, (-1, 1): 5, (1, -1): 6, (1, 1): 7}
+        places = {(-1, 0): 0, (1, 0): 1, (-1, -1): 2, (0, -1): 3, (1, -1): 4, (-1, 1): 5, (0, 1): 6, (1, 1): 7}
 
         def id_at(m, n):
             where = (-1 if m < 0 else int(m >= STRIPS), -1 if n < 0 else int(n >= STRIPS))
@@ -628,19 +631,19 @@
 
 
 def border(tokens, ids, got, rel_index, bias_table, weights, inner):
-    line = 4 * SIDE
     return pl.pallas_call(
         border_kernel,
         grid=(5,),
         out_shape=jax.ShapeDtypeStruct((OUT, OUT, 2 * C), BF16),
-        in_specs=edge_specs()
+        in_specs=row_specs()
+        + col_specs()
         + [whole((STRIPS, SIDE), pltpu.SMEM)]
         + [whole(a.shape) for a in got]
         + [whole(rel_index.shape), whole(bias_table.shape)]
         + [whole(a.shape) for a in weights]
         + [pl.BlockSpec(memory_space=pl.ANY)],
         out_specs=pl.BlockSpec(memory_space=pl.ANY),
-        input_output_aliases={15 + len(weights): 0},
+        input_output_aliases={11 + len(weights): 0},
         scratch_shapes=[
             pltpu.VMEM((VARIANTS, SPOTS, HEADS * SPOTS), F32),
             pltpu.VMEM((C, C), BF16),
@@ -649,7 +652,7 @@
             pltpu.VMEM((16 // GROUP, C, SPOTS * GROUP), BF16),
             pltpu.VMEM((16 * SPOTS, C), F32),
             pltpu.VMEM((4, 16, SPOTS, C), F32),
-            pltpu.VMEM((4 * line + 64, C), F32),
+            pltpu.VMEM((2 * LINE + 2 * BAND, C), F32),
             pltpu.VMEM((8 * STRIPS, SIDE), jnp.int32),
             pltpu.SMEM((8 * STRIPS, SIDE), jnp.int32),
             pltpu.SMEM((4, 16), jnp.int32),
@@ -672,10 +675,17 @@
         norm1_gain.reshape(1, C), w_qkv, w_proj, norm2_gain.reshape(1, C), w_up, w_down,
         merge_gain.reshape(1, 4 * C), w_merge,
     )
-    ids, *messages = pack(tokens, regions)
-    got = exchange(messages)
-    inner = interior(tokens, ids, rel_index, bias_table, weights)
-    return border(tokens, ids, got, rel_index, bias_table, weights, inner)
+    ids, top, bottom = pack_rows(tokens, regions)
+    above, below = moved(bottom, "row", 1), moved(top, "row", -1)
+    inner = interior(tokens, ids, rel_index, bias_table, weights, 0, EARLY)
+    to_left, to_right, token = pack_cols(tokens, above, below, ids, inner)
+    from_left, from_right = moved(to_right, "col", 1), moved(to_left, "col", -1)
+    inner = interior(
+        tokens, ids, rel_index, bias_table, weights, EARLY, SIDE // WIN - 1 - EARLY, before=inner, after=token
+    )
+    return border(
+        tokens, ids, (above, below, from_left, from_right), rel_index, bias_table, weights, inner
+    )
 
 
 def solution(mesh):

time: 112 us -> 94.9 us (0.85)
  waiting for transfers between devices: 22.2 us -> 0.01 us
  Pallas kernels: 73.9 us -> 80 us
  starting transfers between devices: 12.3 us -> 10.6 us
  local copies, waits for them, and re-layouts: 2.16 us -> 3.37 us
    ppermute x8 -> x4, waiting for transfers between devices: 22.2 us -> 0.01 us  [moved(): lax.ppermute(value, axis, [(i, (i + by) % size) for i in range(size)])]
    pallas_call x2 -> x4, Pallas kernels: 53.4 us -> 59.5 us  [the longest x2 55.6 us: interior(): pl.pallas_call(functools.partial(interior_kernel, first, total), grid=(to...]
    ppermute x8 -> x4, starting transfers between devices: 12.3 us -> 10.6 us  [moved(): lax.ppermute(value, axis, [(i, (i + by) % size) for i in range(size)])]
    unnamed x19 -> x11, local copies, waits for them, and re-layouts: 2.16 us -> 3.37 us
  transfers between devices with their start and end apart: 8 -> 4, of which waited for: 3 -> 0; matrix products, arithmetic and copies ran while one was open for 1% -> 1% of each run, Pallas kernels for 46% -> 59%
where the time goes in v2:
time: 94.9 us; the launch traced here: 94.2 us
  Pallas kernels  80 us (84%)
  starting transfers between devices  10.6 us (11%)
  local copies, waits for them, and re-layouts  3.37 us (4%)
    pallas_call x2, Pallas kernels, interior(): pl.pallas_call(functools.partial(interior_kernel, first, total), grid=(to...  55.6 us
    pallas_call x1, Pallas kernels, border(): pl.pallas_call(border_kernel, grid=(5,), out_shape=jax.ShapeDtypeStruct((...  20.4 us
    ppermute x4, starting transfers between devices, moved(): lax.ppermute(value, axis, [(i, (i + by) % size) for i in range(size)])  10.6 us
    unnamed x11, local copies, waits for them, and re-layouts  3.37 us
    pallas_call x1, Pallas kernels, pack_cols(): pl.pallas_call(pack_cols_kernel, grid=(1,), out_shape=[band, band, token]...  2.13 us
  transfers between devices with their start and end apart: 4, of which 0 were waited for; matrix products, arithmetic and copies ran while one was open for 1% of the time, Pallas kernels for 59%

profile of v2, /device:TPU:0, one launch (start us, length us, event | category | flops | bytes accessed | tf_op | source)
XLA Modules:
  0.0 94.2 jit_solution(3992308670372054673)
XLA Ops:
  0.0 0.0 copy-start.4
  0.0 1.8 %shard_map.118 = (s32[8,128]{1,0:T(8,128)}, bf16[528,128]{1,0:T(8,128)(2,1)}, bf16[528,128]{1,0:T(8,128)(2,1)}) custom-call(f32[128,128,128]{2,1,0:T(8,128)} %refs_3_.1, f32[128,128,128]{2,1,0:T(8,128)} %refs_3_.1, s32[128,128]{1,0:T(8,128)} %regions_ref.1), custom_call_target="tpu_custom_call" | custom-call | tf_op jit(solution)/shard_map/pallas_call | solution.py:350
  1.8 0.0 collective-permute-start
  1.8 3.9 %collective-permute-start.1 = (bf16[528,128]{1,0:T(8,128)(2,1)}, bf16[528,128]{1,0:T(8,128)(2,1)S(1)}, u32[]{:S(2)}, u32[]{:S(2)}) collective-permute-start(bf16[528,128]{1,0:T(8,128)(2,1)} %get-tuple-element.13), channel_id=1, source_target_pairs={{0,240},{16,0},{32,16},{48,32},{64,48},{80,64},{96,80},{112,96},{1... | collective-permute-start | bytes 405512 | tf_op jit(solution)/shard_map/ppermute | solution.py:393
  5.6 0.0 copy-done.4
  5.6 0.8 copy.15.table_ref.refs_10_
  6.4 13.9 %shard_map.119.after_ref.refs_8_ = bf16[64,64,256]{2,1,0:T(8,128)(2,1)} custom-call(f32[128,128,128]{2,1,0:T(8,128)} %refs_3_.1, f32[128,128,128]{2,1,0:T(8,128)} %refs_3_.1, s32[8,128]{1,0:T(8,128)} %get-tuple-element.11.ids_ref.refs_4_, s32[64,64]{1,0:T(8,128)} %refs_9_.1, f32[225,4]{1,0:T(8,128)} %copy.15.table_ref.refs_10_, f32[1,128]{1,0:T(1,128)} %bitcast.6, ...), custom_call_target="tpu_custom_call" | custom-call | tf_op jit(solution)/shard_map/pallas_call | solution.py:289
  20.3 0.0 collective-permute-done.above_ref.refs_5_
  20.3 0.0 copy-start
  20.3 0.0 collective-permute-done.1.below_ref.refs_6_
  20.3 0.6 copy-done
  20.9 0.0 copy-start.1
  20.9 0.6 copy-done.1
  21.6 2.1 %shard_map.120 = (bf16[592,128]{1,0:T(8,128)(2,1)}, bf16[592,128]{1,0:T(8,128)(2,1)}, f32[8,128]{1,0:T(8,128)}) custom-call(f32[128,128,128]{2,1,0:T(8,128)} %refs_3_.1, f32[128,128,128]{2,1,0:T(8,128)} %refs_3_.1, bf16[528,128]{1,0:T(8,128)(2,1)} %copy-done, bf16[528,128]{1,0:T(8,128)(2,1)} %copy-done.1, s32[8,128]{1,0:T(8,128)} %get-tuple-element.11.ids_ref.refs_4_, ...), custom_call_target="tpu_custom_call" | custom-call | tf_op jit(solution)/shard_map/pallas_call | solution.py:380
  23.7 1.5 %collective-permute-start.2 = (bf16[592,128]{1,0:T(8,128)(2,1)}, bf16[592,128]{1,0:T(8,128)(2,1)S(1)}, u32[]{:S(2)}, u32[]{:S(2)}) collective-permute-start(bf16[592,128]{1,0:T(8,128)(2,1)} %get-tuple-element.14), channel_id=1, source_target_pairs={{0,1},{1,2},{2,3},{3,4},{4,5},{5,6},{6,7},{7,8},{8,9},{9,10},{10,1... | collective-permute-start | bytes 454664 | tf_op jit(solution)/shard_map/ppermute | solution.py:393
  25.2 5.3 %collective-permute-start.3 = (bf16[592,128]{1,0:T(8,128)(2,1)}, bf16[592,128]{1,0:T(8,128)(2,1)S(1)}, u32[]{:S(2)}, u32[]{:S(2)}) collective-permute-start(bf16[592,128]{1,0:T(8,128)(2,1)} %get-tuple-element.15), channel_id=1, source_target_pairs={{0,15},{1,0},{2,1},{3,2},{4,3},{5,4},{6,5},{7,6},{8,7},{9,8},{10,9... | collective-permute-start | bytes 454664 | tf_op jit(solution)/shard_map/ppermute | solution.py:393
  30.5 41.8 %shard_map.121.refs_19_ = bf16[64,64,256]{2,1,0:T(8,128)(2,1)} custom-call(f32[128,128,128]{2,1,0:T(8,128)} %refs_3_.1, f32[128,128,128]{2,1,0:T(8,128)} %refs_3_.1, s32[8,128]{1,0:T(8,128)} %get-tuple-element.11.ids_ref.refs_4_, s32[64,64]{1,0:T(8,128)} %refs_9_.1, f32[225,4]{1,0:T(8,128)} %copy.15.table_ref.refs_10_, ...), custom_call_target="tpu_custom_call", output_to_operand_aliasing={{}: (13, {})} | custom-call | tf_op jit(solution)/shard_map/pallas_call | solution.py:289
  72.2 0.0 collective-permute-done.2.refs_7_
  72.2 0.0 copy-start.2
  72.2 0.0 collective-permute-done.3.refs_8_
  72.3 0.6 copy-done.2
  72.9 0.0 copy-start.3
  72.9 0.7 copy-done.3
  73.5 20.4 %shard_map.122 = bf16[64,64,256]{2,1,0:T(8,128)(2,1)} custom-call(f32[128,128,128]{2,1,0:T(8,128)} %refs_3_.1, f32[128,128,128]{2,1,0:T(8,128)} %refs_3_.1, f32[128,128,128]{2,1,0:T(8,128)} %refs_3_.1, f32[128,128,128]{2,1,0:T(8,128)} %refs_3_.1, s32[8,128]{1,0:T(8,128)} %get-tuple-element.11.ids_ref.refs_4_, ...), custom_call_target="tpu_custom_call", output_to_operand_aliasing={{}: (19, {})} | custom-call | tf_op jit(solution)/shard_map/pallas_call | solution.py:634
Async XLA Ops:
  0.0 5.6 %copy-start.4 = (f32[225,4]{0,1:T(4,128)S(1)}, f32[225,4]{0,1:T(4,128)}, u32[]{:S(2)}) copy-start(f32[225,4]{0,1:T(4,128)} %param.15) | copy-start | bytes 10804
  1.8 18.5 %collective-permute-start = (bf16[528,128]{1,0:T(8,128)(2,1)}, bf16[528,128]{1,0:T(8,128)(2,1)S(1)}, u32[]{:S(2)}, u32[]{:S(2)}) collective-permute-start(bf16[528,128]{1,0:T(8,128)(2,1)} %get-tuple-element.12), channel_id=1, source_target_pairs={{0,16},{16,32},{32,48},{48,64},{64,80},{80,96},{96,112},{112,128},... | collective-permute-start | bytes 405512 | tf_op jit(solution)/shard_map/ppermute | solution.py:393
  1.8 18.5 %collective-permute-start.1 = (bf16[528,128]{1,0:T(8,128)(2,1)}, bf16[528,128]{1,0:T(8,128)(2,1)S(1)}, u32[]{:S(2)}, u32[]{:S(2)}) collective-permute-start(bf16[528,128]{1,0:T(8,128)(2,1)} %get-tuple-element.13), channel_id=1, source_target_pairs={{0,240},{16,0},{32,16},{48,32},{64,48},{80,64},{96,80},{112,96},{1... | collective-permute-start | bytes 405512 | tf_op jit(solution)/shard_map/ppermute | solution.py:393
  20.3 0.7 copy-start
  20.9 0.6 copy-start.1
  23.7 48.5 %collective-permute-start.2 = (bf16[592,128]{1,0:T(8,128)(2,1)}, bf16[592,128]{1,0:T(8,128)(2,1)S(1)}, u32[]{:S(2)}, u32[]{:S(2)}) collective-permute-start(bf16[592,128]{1,0:T(8,128)(2,1)} %get-tuple-element.14), channel_id=1, source_target_pairs={{0,1},{1,2},{2,3},{3,4},{4,5},{5,6},{6,7},{7,8},{8,9},{9,10},{10,1... | collective-permute-start | bytes 454664 | tf_op jit(solution)/shard_map/ppermute | solution.py:393
  25.2 47.1 %collective-permute-start.3 = (bf16[592,128]{1,0:T(8,128)(2,1)}, bf16[592,128]{1,0:T(8,128)(2,1)S(1)}, u32[]{:S(2)}, u32[]{:S(2)}) collective-permute-start(bf16[592,128]{1,0:T(8,128)(2,1)} %get-tuple-element.15), channel_id=1, source_target_pairs={{0,15},{1,0},{2,1},{3,2},{4,3},{5,4},{6,5},{7,6},{8,7},{9,8},{10,9... | collective-permute-start | bytes 454664 | tf_op jit(solution)/shard_map/ppermute | solution.py:393
  72.2 0.7 copy-start.2
  72.9 0.7 copy-start.3

commit v3 on v2

--- a/solution.py
+++ b/solution.py
@@ -42,47 +42,103 @@
     return h + h * jnp.tanh(inner)
 
 
-def prepare(rel_ref, table_ref, w_qkv_ref, w_up_ref, bias_scr, wvt_scr, wup_scr, pad_scr):
+def prepare_weights(table_ref, w_qkv_ref, w_up_ref, wvt_scr, wup_scr, pad_scr):
     wvt_scr[...] = w_qkv_ref[:, 2 * C :].astype(F32).T.astype(BF16)
     wup_scr[...] = w_up_ref[...] * jnp.asarray(0.5, BF16)
     pad_scr[...] = jnp.zeros_like(pad_scr)
-    pad_scr[pl.ds(0, table_ref.shape[0]), pl.ds(0, HEADS)] = table_ref[...]
-    table_a = pad_scr[pl.ds(0, 128), :].T
-    table_b = pad_scr[pl.ds(128, 128), :].T
+    rest = table_ref.shape[1] - 128
+    pad_scr[pl.ds(128, HEADS), :] = table_ref[:, :128]
+    pad_scr[pl.ds(136, HEADS), pl.ds(0, rest)] = table_ref[:, 128:]
+
+
+def from_table(rel, head, pad_scr):
+    low = rel < 128
+    spot = jnp.where(low, rel, rel - 128)
+    got = []
+    for first in (128, 136):
+        row = jnp.broadcast_to(pad_scr[pl.ds(first + head, 1), :], rel.shape)
+        got.append(jnp.take_along_axis(row, spot, axis=1, mode="promise_in_bounds"))
+    return jnp.where(low, got[0], got[1]) * LOG2E
+
+
+def fill_variants(bias_scr, first, bias, key_quarter, query_quarter):
+    def label_of(quarter, labels):
+        return jnp.where(
+            quarter == 0, 0, jnp.where(quarter == 1, labels[0], jnp.where(quarter == 2, labels[1], labels[2]))
+        )
+
+    for one in range(2):
+        for two in (0, 1, 2) if one else (0, 2):
+            for three in range(4):
+                if (three == 1 and not one) or (three == 2 and two != 2):
+                    continue
+                same = label_of(key_quarter, (one, two, three)) == label_of(query_quarter, (one, two, three))
+                bias_scr[first + one * 12 + two * 4 + three] = jnp.where(same, bias, -1e30)
+
+
+def prepare(rel_ref, table_ref, w_qkv_ref, w_up_ref, bias_scr, wvt_scr, wup_scr, pad_scr):
+    prepare_weights(table_ref, w_qkv_ref, w_up_ref, wvt_scr, wup_scr, pad_scr)
     pad_scr[pl.ds(0, SPOTS), pl.ds(0, SPOTS)] = rel_ref[...].astype(F32)
     rel_t = pad_scr[pl.ds(0, 128), :].T[:SPOTS, :].astype(jnp.int32)
-    rel_t = jnp.where(lax.broadcasted_iota(jnp.int32, (SPOTS, 128), 1) < SPOTS, rel_t, pltpu.roll(rel_t, SPOTS, 1))
-    low = rel_t < 128
-    spot = jnp.where(low, rel_t, rel_t - 128)
     lane = lax.broadcasted_iota(jnp.int32, (SPOTS, 128), 1)
+    rel_t = jnp.where(lane < SPOTS, rel_t, pltpu.roll(rel_t, SPOTS, 1))
     halves = []
     for pair in range(HEADS // 2):
-        per_head = []
-        for head in (2 * pair, 2 * pair + 1):
-            row_a = jnp.broadcast_to(table_a[head : head + 1, :], (SPOTS, 128))
-            row_b = jnp.broadcast_to(table_b[head : head + 1, :], (SPOTS, 128))
-            got_a = jnp.take_along_axis(row_a, spot, axis=1, mode="promise_in_bounds")
-            got_b = jnp.take_along_axis(row_b, spot, axis=1, mode="promise_in_bounds")
-            per_head.append(jnp.where(low, got_a, got_b))
-        halves.append(jnp.where(lane < SPOTS, per_head[0], per_head[1]) * LOG2E)
-    bias = jnp.concatenate(halves, axis=1)
-    key_spot = lax.broadcasted_iota(jnp.int32, (SPOTS, 2 * 128), 0)
-    query_spot = lax.broadcasted_iota(jnp.int32, (SPOTS, 2 * 128), 1) % SPOTS
-
-    def label_of(spots, labels):
-        right = (spots % WIN) >= WIN // 2
-        lower = spots >= SPOTS // 2
-        top = jnp.where(right, labels[0], 0)
-        low_row = jnp.where(right, labels[2], labels[1])
-        return jnp.where(lower, low_row, top)
-
-    def variant(index, carry):
-        labels = (index // 12, (index // 4) % 3, index % 4)
-        same = label_of(key_spot, labels) == label_of(query_spot, labels)
-        bias_scr[index] = jnp.where(same, bias, -1e30)
-        return carry
-
-    lax.fori_loop(0, VARIANTS, variant, 0)
+        per_head = [from_table(rel_t, head, pad_scr) for head in (2 * pair, 2 * pair + 1)]
+        halves.append(jnp.where(lane < SPOTS, per_head[0], per_head[1]))
+
+    def quarter(spots):
+        return spots // 32 * 2 + spots % WIN // 4
+
+    fill_variants(
+        bias_scr,
+        0,
+        jnp.concatenate(halves, axis=1),
+        quarter(lax.broadcasted_iota(jnp.int32, (SPOTS, 1), 0)),
+        quarter(lax.broadcasted_iota(jnp.int32, (1, 2 * 128), 1) % SPOTS),
+    )
+
+
+def border_spot(strip, spot):
+    if strip in (0, 2):
+        return (spot + 32 * (strip == 0)) % SPOTS
+    half, y, x = spot // 32, spot % 32 // 4, spot % 4
+    return y * WIN + (half if strip == 1 else 1 - half) * 4 + x
+
+
+def border_quarter(strip, spots):
+    half = spots // 32
+    if strip == 0:
+        return (1 - half) * 2 + spots % WIN // 4
+    if strip == 2:
+        return half * 2 + spots % WIN // 4
+    return spots % 32 // 16 * 2 + (half if strip == 1 else 1 - half)
+
+
+def prepare_border(rel_ref, table_ref, w_qkv_ref, w_up_ref, bias_scr, wvt_scr, wup_scr, pad_scr, turn_scr):
+    prepare_weights(table_ref, w_qkv_ref, w_up_ref, wvt_scr, wup_scr, pad_scr)
+    lane = lax.broadcasted_iota(jnp.int32, (SPOTS, 128), 1)
+    turn_scr[...] = jnp.zeros_like(turn_scr)
+    for strip in range(4):
+        for at in range(0, SPOTS, 4):
+            pad_scr[pl.ds(at, 4), pl.ds(0, SPOTS)] = rel_ref[pl.ds(border_spot(strip, at), 4), :].astype(F32)
+        turn_scr[...] = pad_scr[pl.ds(0, 128), :].T
+        rel_t = jnp.concatenate(
+            [turn_scr[pl.ds(border_spot(strip, at), 4), :] for at in range(0, SPOTS, 4)], axis=0
+        )
+        rel_t = jnp.where(lane < 32, rel_t, 0.0)
+        rel_t = rel_t + pltpu.roll(rel_t, 32, 1)
+        rel_t = (rel_t + pltpu.roll(rel_t, 64, 1)).astype(jnp.int32)
+        bias = from_table(rel_t, 0, pad_scr)
+        for head in range(1, HEADS):
+            bias = jnp.where(lane // 32 == head, from_table(rel_t, head, pad_scr), bias)
+        fill_variants(
+            bias_scr,
+            VARIANTS * strip,
+            bias,
+            border_quarter(strip, lax.broadcasted_iota(jnp.int32, (SPOTS, 1), 0)),
+            border_quarter(strip, lax.broadcasted_iota(jnp.int32, (1, 128), 1) % 32),
+        )
 
 
 def pattern(top_left, top_right, low_left, low_right):
@@ -96,23 +152,34 @@
     return one * 12 + two * 4 + three
 
 
-def front(loads, store_att, variants, w, bias_scr, wvt_scr):
-    normed = []
-    for load in loads:
-        normed.append(layer_norm(load(), w["g1"][...]).astype(BF16))
+def front(loads, store_att, variants, w, bias_scr, wvt_scr, base, nrm_scr, q_scr, k_scr, vt_scr, nq=SPOTS):
+    for i, load in enumerate(loads):
+        nrm_scr[pl.ds(base + SPOTS * i, SPOTS), :] = layer_norm(load(), w["g1"][...]).astype(BF16)
         yield
-    normed = jnp.concatenate(normed, axis=0)
-    qk = jnp.dot(normed, w["w_qkv"][:, : 2 * C], preferred_element_type=F32)
-    vt = lax.dot_general(wvt_scr[...], normed, NT, preferred_element_type=F32).astype(BF16)
+    size = SPOTS * len(loads)
+    for at in range(0, size, QPIECE):
+        piece = min(QPIECE, size - at)
+        rows = pl.ds(base + at, piece)
+        qk = jnp.dot(nrm_scr[rows, :], w["w_qkv"][:, : 2 * C], preferred_element_type=F32)
+        for i in range(0, piece, SPOTS):
+            part = qk[i : i + SPOTS]
+            q_scr[pl.ds(base + at + i, SPOTS), :] = (part[:, :C] * QSCALE).astype(BF16)
+            k_scr[pl.ds(base + at + i, SPOTS), :] = part[:, C:].astype(BF16)
+        yield
+    for at in range(0, size, 256):
+        wide = min(256, size - at)
+        vt_scr[:, pl.ds(base + at, wide)] = lax.dot_general(
+            wvt_scr[...], nrm_scr[pl.ds(base + at, wide), :], NT, preferred_element_type=F32
+        ).astype(BF16)
     yield
     lane = lax.broadcasted_iota(jnp.int32, (1, C), 1)
     n = len(loads)
     st, ot = {}, {}
     for i in range(n + 2 * LAG):
         if i < n:
-            rows = slice(SPOTS * i, SPOTS * (i + 1))
-            q = (qk[rows, :C] * QSCALE).astype(BF16)
-            k = qk[rows, C:].astype(BF16)
+            rows = pl.ds(base + SPOTS * i, SPOTS)
+            q = q_scr[pl.ds(base + SPOTS * i, nq), :]
+            k = k_scr[rows, :]
             qm = jnp.concatenate([jnp.where(lane // HD == h, q, jnp.zeros_like(q)) for h in range(HEADS)], axis=0)
             st[i] = lax.dot_general(k, qm, NT, preferred_element_type=F32)
         at = i - LAG
@@ -121,7 +188,7 @@
             scores = st.pop(at) + bias_scr[variants[at]]
             top = jnp.max(scores, axis=0, keepdims=True)
             p = jnp.exp2((scores - top).astype(BF16))
-            vw = jnp.concatenate([vt[:, rows], jnp.ones((16, SPOTS), BF16)], axis=0)
+            vw = jnp.concatenate([vt_scr[:, pl.ds(base + SPOTS * at, SPOTS)], jnp.ones((16, SPOTS), BF16)], axis=0)
             ot[at] = jnp.dot(vw, p, preferred_element_type=F32)
         at = i - 2 * LAG
         if 0 <= at < n:
@@ -131,8 +198,8 @@
                 at,
                 jnp.concatenate(
                     [
-                        got[HD * h : HD * (h + 1), SPOTS * h : SPOTS * (h + 1)]
-                        * inv[:, SPOTS * h : SPOTS * (h + 1)]
+                        got[HD * h : HD * (h + 1), nq * h : nq * (h + 1)]
+                        * inv[:, nq * h : nq * (h + 1)]
                         for h in range(HEADS)
                     ],
                     axis=0,
@@ -141,28 +208,34 @@
         yield
 
 
-def back(loads, load_att, stores, w, wup_scr):
+def back(loads, load_att, stores, w, wup_scr, base, mid_scr, sec_scr, wide_scr, nq=SPOTS):
+    size = nq * len(loads)
     proj = lax.dot_general(load_att(), w["w_proj"][...], TN, preferred_element_type=F32)
     yield
-    mids, second = [], []
     for i, load in enumerate(loads):
-        mids.append(load() + proj[SPOTS * i : SPOTS * (i + 1)])
-        second.append(layer_norm(mids[-1], w["g2"][...]).astype(BF16))
+        rows = pl.ds(base + nq * i, nq)
+        mid = load() + proj[nq * i : nq * (i + 1)]
+        mid_scr[rows, :] = mid
+        sec_scr[rows, :] = layer_norm(mid, w["g2"][...]).astype(BF16)
         yield
-    up = jnp.dot(jnp.concatenate(second, axis=0), wup_scr[...], preferred_element_type=F32)
-    yield
-    wide = []
-    for i in range(len(loads)):
-        wide.append(half_gelu(up[SPOTS * i : SPOTS * (i + 1)]))
+    for at in range(0, size, PIECE):
+        piece = min(PIECE, size - at)
+        up = jnp.dot(sec_scr[pl.ds(base + at, piece), :], wup_scr[...], preferred_element_type=F32)
         yield
-    down = jnp.dot(jnp.concatenate(wide, axis=0), w["w_down"][...], preferred_element_type=F32)
+        for i in range(0, piece, 32):
+            wide_scr[pl.ds(base + at + i, 32), :] = half_gelu(up[i : i + 32])
+            if i % 64:
+                yield
+    down = jnp.dot(wide_scr[pl.ds(base, size), :], w["w_down"][...], preferred_element_type=F32)
     yield
     for i, store in enumerate(stores):
-        store(mids[i] + down[SPOTS * i : SPOTS * (i + 1)])
+        store(mid_scr[pl.ds(base + nq * i, nq), :] + down[nq * i : nq * (i + 1)])
         yield
 
 
-LAG = 2
+PIECE = 256
+QPIECE = 256
+LAG = 1
 
 
 def merge(load_parts, store, w):
@@ -185,14 +258,17 @@
 
 NAMES = ("g1", "w_qkv", "w_proj", "g2", "w_up", "w_down", "gm", "w_merge")
 GROUP = 8
+FRONT_AT = 0
 FRONT_EVERY, FRONT_GAP = 20, 1
 BACK_EVERY, BACK_GAP = 16, 0.8
+BORDER_FRONT_EVERY, BORDER_BACK_EVERY = 10, 12
 MERGE_EVERY, MERGE_GAP, MERGE_AT = 1.0, 1.0, 50
 
 
 def interior_kernel(first, total, x_ref, old_ref, ids_ref, rel_ref, table_ref, *refs):
     w = dict(zip(NAMES, refs[:8]))
-    out_ref, bias_scr, wvt_scr, wup_scr, pad_scr, att_scr, blk_scr = refs[-7:]
+    out_ref = refs[-14]
+    (bias_scr, wvt_scr, wup_scr, pad_scr, att_scr, blk_scr, nrm_scr, q_scr, k_scr, vt_scr, mid_scr, sec_scr, wide_scr) = refs[-13:]
     step = pl.program_id(0)
     count = SIDE // WIN - 1
 
@@ -229,9 +305,9 @@
     def fronts():
         return [
             (
-                FRONT_EVERY * g,
+                FRONT_AT + FRONT_EVERY * g,
                 FRONT_GAP,
-                front([loader(x_ref, j) for j in js], store_att(g), [variant(j) for j in js], w, bias_scr, wvt_scr),
+                front([loader(x_ref, j) for j in js], store_att(g), [variant(j) for j in js], w, bias_scr, wvt_scr, SPOTS * js[0], nrm_scr, q_scr, k_scr, vt_scr),
             )
             for g, js in enumerate(groups)
         ]
@@ -247,6 +323,10 @@
                     [store_block(j) for j in js],
                     w,
                     wup_scr,
+                    SPOTS * js[0],
+                    mid_scr,
+                    sec_scr,
+                    wide_scr,
                 ),
             )
             for g, js in enumerate(groups)
@@ -311,8 +391,15 @@
             pltpu.VMEM((256, 128), F32),
             pltpu.VMEM((groups, C, SPOTS * GROUP), BF16),
             pltpu.VMEM((WIN, SIDE, C), F32),
+            pltpu.VMEM((16 * SPOTS, C), BF16),
+            pltpu.VMEM((16 * SPOTS, C), BF16),
+            pltpu.VMEM((16 * SPOTS, C), BF16),
+            pltpu.VMEM((C, 16 * SPOTS), BF16),
+            pltpu.VMEM((16 * SPOTS, C), F32),
+            pltpu.VMEM((16 * SPOTS, C), BF16),
+            pltpu.VMEM((16 * SPOTS, MLP), BF16),
         ],
-        compiler_params=pltpu.CompilerParams(vmem_limit_bytes=56 * 1024 * 1024),
+        compiler_params=pltpu.CompilerParams(vmem_limit_bytes=18 * 1024 * 1024),
     )(*args)
 
 
@@ -353,10 +440,22 @@
         out_shape=shapes,
         in_specs=row_specs() + [whole((SIDE, SIDE))],
         out_specs=[whole(a.shape) for a in shapes],
+        compiler_params=pltpu.CompilerParams(vmem_limit_bytes=16 * 1024 * 1024),
     )(tokens, tokens, regions)
 
 
-def pack_cols_kernel(left_ref, right_ref, above_ref, below_ref, ids_ref, after_ref, to_left, to_right, token_ref, band_scr, row_scr):
+def pack_cols_kernel(
+    left_ref, right_ref, above_any, below_any, ids_ref, after_ref, to_left, to_right, token_ref, band_scr, row_scr,
+    above_ref, below_ref, sems,
+):
+    copies = [
+        pltpu.make_async_copy(above_any, above_ref, sems.at[0]),
+        pltpu.make_async_copy(below_any, below_ref, sems.at[1]),
+    ]
+    for copy in copies:
+        copy.start()
+    for copy in copies:
+        copy.wait()
     token_ref[...] = jnp.zeros_like(token_ref)
     row_scr[0] = above_ref[pl.ds(0, LINE), :].astype(F32)
     row_scr[1] = below_ref[pl.ds(0, LINE), :].astype(F32)
@@ -382,9 +481,17 @@
         grid=(1,),
         out_shape=[band, band, token],
         in_specs=col_specs()
-        + [whole(above.shape), whole(below.shape), whole(ids.shape), pl.BlockSpec(memory_space=pl.ANY)],
+        + [pl.BlockSpec(memory_space=pl.ANY)] * 2
+        + [whole(ids.shape), pl.BlockSpec(memory_space=pl.ANY)],
         out_specs=[whole(band.shape), whole(band.shape), whole(token.shape)],
-        scratch_shapes=[pltpu.VMEM((BAND, C), F32), pltpu.VMEM((2, LINE, C), F32)],
+        scratch_shapes=[
+            pltpu.VMEM((BAND, C), F32),
+            pltpu.VMEM((2, LINE, C), F32),
+            pltpu.VMEM(above.shape, BF16),
+            pltpu.VMEM(below.shape, BF16),
+            pltpu.SemaphoreType.DMA((2,)),
+        ],
+        compiler_params=pltpu.CompilerParams(vmem_limit_bytes=16 * 1024 * 1024),
     )(tokens, tokens, above, below, ids, after)
 
 
@@ -412,14 +519,15 @@
     above, below, from_left, from_right = row_of(0), row_of(1), col_of(0), col_of(1)
     for t in range(16):
         for y in range(8):
-            spot = WIN * y
+            turned, spot = WIN * ((y + 4) % 8), WIN * y
+            first, second = 4 * y, 32 + 4 * y
             side, at = (above, y) if y < 4 else (own(top), y - 4)
             if t == 0:
                 edge = from_left(y - 4, 0, 4)
-                x_scr[0, t, pl.ds(spot, 4), :] = edge
-                x_scr[0, t, pl.ds(spot + 4, 4), :] = side(at, 0, 4)
+                x_scr[0, t, pl.ds(turned, 4), :] = edge
+                x_scr[0, t, pl.ds(turned + 4, 4), :] = side(at, 0, 4)
             else:
-                x_scr[0, t, pl.ds(spot, 8), :] = side(at, 8 * t - 4, 8)
+                x_scr[0, t, pl.ds(turned, 8), :] = side(at, 8 * t - 4, 8)
             side, at = (own(bottom), y) if y < 4 else (below, y - 4)
             if t == 15:
                 edge = from_right(124 + y, 0, 4)
@@ -428,11 +536,11 @@
             else:
                 x_scr[2, t, pl.ds(spot, 8), :] = side(at, 8 * t + 4, 8)
             r = 8 * t - 4 + y
-            x_scr[1, t, pl.ds(spot, 4), :] = above(y, 124, 4) if r < 0 else own(right)(r, 4, 4)
-            x_scr[1, t, pl.ds(spot + 4, 4), :] = from_right(r, 0, 4)
+            x_scr[1, t, pl.ds(first, 4), :] = above(y, 124, 4) if r < 0 else own(right)(r, 4, 4)
+            x_scr[1, t, pl.ds(second, 4), :] = from_right(r, 0, 4)
             r = 8 * t + 4 + y
-            x_scr[3, t, pl.ds(spot, 4), :] = from_left(r, 0, 4)
-            x_scr[3, t, pl.ds(spot + 4, 4), :] = below(r - SIDE, 0, 4) if r >= SIDE else own(left)(r, 0, 4)
+            x_scr[3, t, pl.ds(second, 4), :] = from_left(r, 0, 4)
+            x_scr[3, t, pl.ds(first, 4), :] = below(r - SIDE, 0, 4) if r >= SIDE else own(left)(r, 0, 4)
 
 
 def border_patterns(id_at, var_smem):
@@ -445,12 +553,12 @@
 
 
 def border_kernel(*refs):
-    edges, own_ids, got = refs[:4], refs[4], refs[5:9]
+    edges, own_ids, got_any = refs[:4], refs[4], refs[5:9]
     rel_ref, table_ref = refs[9:11]
     w = dict(zip(NAMES, refs[11:19]))
     inner_ref, out_ref = refs[19:21]
     (bias_scr, wvt_scr, wup_scr, pad_scr, att_scr, blk_scr, x_scr, msg_scr, idv_scr, ids_smem, var_smem, row_scr,
-     col_scr, row_out, col_out, sem_ids, sem_in, sem_out) = refs[21:]
+     col_scr, row_out, col_out, sem_ids, sem_in, sem_out, got_a, got_b, got_c, got_d, sem_got, nrm_scr, q_scr, k_scr, vt_scr, mid_scr, sec_scr, wide_scr, turn_scr) = refs[21:]
     step = pl.program_id(0)
     count = 16
     col_in = [
@@ -460,8 +568,15 @@
 
     @pl.when(step == 0)
     def _():
-        for copy in col_in:
+        got = (got_a, got_b, got_c, got_d)
+        arrive = [pltpu.make_async_copy(got_any[n], got[n], sem_got.at[n]) for n in range(4)]
+        for copy in arrive + col_in:
             copy.start()
+        prepare_border(
+            rel_ref, table_ref, w["w_qkv"], w["w_up"], bias_scr, wvt_scr, wup_scr, pad_scr, turn_scr
+        )
+        for copy in arrive:
+            copy.wait()
         places = [(0, LINE), (1, LINE)]
         places += [(2 + side, BAND + IDROWS * m) for side in range(2) for m in range(3)]
         for n, (source, first) in enumerate(places):
@@ -471,7 +586,6 @@
         ids_copy = pltpu.make_async_copy(idv_scr, ids_smem, sem_ids)
         ids_copy.start()
         gather_border(edges, got, x_scr, msg_scr)
-        prepare(rel_ref, table_ref, w["w_qkv"], w["w_up"], bias_scr, wvt_scr, wup_scr, pad_scr)
         ids_copy.wait()
         places = {(-1, 0): 0, (1, 0): 1, (-1, -1): 2, (0, -1): 3, (1, -1): 4, (-1, 1): 5, (0, 1): 6, (1, 1): 7}
 
@@ -488,28 +602,32 @@
 
     def store_att(g):
         def store(i, value):
-            att_scr[g, :, pl.ds(SPOTS * i, SPOTS)] = value
+            att_scr[g, :, pl.ds(32 * i, 32)] = value
 
         return store
 
     def store_block(t):
         def store(value):
-            blk_scr[pl.ds(SPOTS * t, SPOTS), :] = value
+            blk_scr[pl.ds(32 * t, 32), :] = value
 
         return store
 
     def fronts():
         return [
             (
-                FRONT_EVERY * g,
+                BORDER_FRONT_EVERY * g,
                 FRONT_GAP,
                 front(
                     [lambda t=t: x_scr[step, t] for t in ts],
                     store_att(g),
-                    [var_smem[step, t] for t in ts],
+                    [VARIANTS * step + var_smem[step, t] for t in ts],
                     w,
                     bias_scr,
                     wvt_scr,
+                    SPOTS * ts[0],
+                    nrm_scr, q_scr, k_scr,
+                    vt_scr,
+                    nq=32,
                 ),
             )
             for g, ts in enumerate(groups)
@@ -518,14 +636,19 @@
     def backs():
         return [
             (
-                BACK_EVERY * g,
+                BORDER_BACK_EVERY * g,
                 BACK_GAP,
                 back(
-                    [lambda t=t: x_scr[step - 1, t] for t in ts],
+                    [lambda t=t: x_scr[step - 1, t, pl.ds(0, 32), :] for t in ts],
                     lambda g=g: att_scr[g],
                     [store_block(t) for t in ts],
                     w,
                     wup_scr,
+                    32 * ts[0],
+                    mid_scr,
+                    sec_scr,
+                    wide_scr,
+                    nq=32,
                 ),
             )
             for g, ts in enumerate(groups)
@@ -550,50 +673,46 @@
     def both(scr, at, rows):
         return jnp.concatenate([scr[2 * at + half, rows, :] for half in range(2)], axis=1)
 
-    @pl.when(step > 0)
-    def _():
-        results = {}
-        for a in range(4):
-            joined = []
-            for dx in range(2):
-                for dy in range(2):
-                    joined.append(
-                        jnp.concatenate(
-                            [
-                                blk_scr[pl.ds((2 * a + dy) * WIN + 2 * b + dx, count, stride=SPOTS), :]
-                                for b in range(4)
-                            ],
-                            axis=0,
-                        )
-                    )
-            normed = layer_norm(jnp.concatenate(joined, axis=1), w["gm"][...]).astype(BF16)
-            merged = jnp.dot(normed, w["w_merge"][...], preferred_element_type=F32)
-            for b in range(4):
-                results[a, b] = merged[count * b : count * (b + 1)]
-
-        @pl.when(step == 1)
-        def _():
-            for a in (2, 3):
-                for b in range(4):
-                    spread(row_scr, a - 2, 8 + b - 2, results[a, b])
-
-        @pl.when(step == 2)
-        def _():
-            for b in (0, 1):
-                for a in range(4):
-                    spread(col_scr, 2 + b, 8 + a - 2, results[a, b])
-
-        @pl.when(step == 3)
-        def _():
-            for a in (0, 1):
-                for b in range(4):
-                    spread(row_scr, 2 + a, 8 + b + 2, results[a, b])
-
-        @pl.when(step == 4)
-        def _():
-            for b in (2, 3):
-                for a in range(4):
-                    spread(col_scr, b - 2, 8 + a + 2, results[a, b])
+    def merged(spots):
+        joined = [
+            jnp.concatenate([blk_scr[pl.ds(four[n], count, stride=32), :] for four in spots], axis=0)
+            for n in range(4)
+        ]
+        normed = layer_norm(jnp.concatenate(joined, axis=1), w["gm"][...]).astype(BF16)
+        out = jnp.dot(normed, w["w_merge"][...], preferred_element_type=F32)
+        return [out[count * n : count * (n + 1)] for n in range(len(spots))]
+
+    def row_merged():
+        for a in range(2):
+            fours = [[(2 * a + dy) * WIN + 2 * b + dx for dx in range(2) for dy in range(2)] for b in range(4)]
+            for b, value in enumerate(merged(fours)):
+                yield a, b, value
+
+    def col_merged():
+        for b in range(2):
+            fours = [[(2 * a + dy) * 4 + 2 * b + dx for dx in range(2) for dy in range(2)] for a in range(4)]
+            for a, value in enumerate(merged(fours)):
+                yield a, b, value
+
+    @pl.when(step == 1)
+    def _():
+        for a, b, value in row_merged():
+            spread(row_scr, a, 8 + b - 2, value)
+
+    @pl.when(step == 2)
+    def _():
+        for a, b, value in col_merged():
+            spread(col_scr, 2 + b, 8 + a - 2, value)
+
+    @pl.when(step == 3)
+    def _():
+        for a, b, value in row_merged():
+            spread(row_scr, 2 + a, 8 + b + 2, value)
+
+    @pl.when(step == 4)
+    def _():
+        for a, b, value in col_merged():
+            spread(col_scr, b, 8 + a + 2, value)
 
     @pl.when(step == 4)
     def _():
@@ -638,18 +757,18 @@
         in_specs=row_specs()
         + col_specs()
         + [whole((STRIPS, SIDE), pltpu.SMEM)]
-        + [whole(a.shape) for a in got]
+        + [pl.BlockSpec(memory_space=pl.ANY) for _ in got]
         + [whole(rel_index.shape), whole(bias_table.shape)]
         + [whole(a.shape) for a in weights]
         + [pl.BlockSpec(memory_space=pl.ANY)],
         out_specs=pl.BlockSpec(memory_space=pl.ANY),
         input_output_aliases={11 + len(weights): 0},
         scratch_shapes=[
-            pltpu.VMEM((VARIANTS, SPOTS, HEADS * SPOTS), F32),
+            pltpu.VMEM((4 * VARIANTS, SPOTS, HEADS * 32), F32),
             pltpu.VMEM((C, C), BF16),
             pltpu.VMEM((C, MLP), BF16),
             pltpu.VMEM((256, 128), F32),
-            pltpu.VMEM((16 // GROUP, C, SPOTS * GROUP), BF16),
+            pltpu.VMEM((16 // GROUP, C, 32 * GROUP), BF16),
             pltpu.VMEM((16 * SPOTS, C), F32),
             pltpu.VMEM((4, 16, SPOTS, C), F32),
             pltpu.VMEM((2 * LINE + 2 * BAND, C), F32),
@@ -663,8 +782,18 @@
             pltpu.SemaphoreType.DMA,
             pltpu.SemaphoreType.DMA((2,)),
             pltpu.SemaphoreType.DMA((4,)),
+            *[pltpu.VMEM(a.shape, BF16) for a in got],
+            pltpu.SemaphoreType.DMA((4,)),
+            pltpu.VMEM((16 * SPOTS, C), BF16),
+            pltpu.VMEM((16 * SPOTS, C), BF16),
+            pltpu.VMEM((16 * SPOTS, C), BF16),
+            pltpu.VMEM((C, 16 * SPOTS), BF16),
+            pltpu.VMEM((16 * SPOTS, C), F32),
+            pltpu.VMEM((16 * SPOTS, C), BF16),
+            pltpu.VMEM((16 * SPOTS, MLP), BF16),
+            pltpu.VMEM((128, 128), F32),
         ],
-        compiler_params=pltpu.CompilerParams(vmem_limit_bytes=56 * 1024 * 1024),
+        compiler_params=pltpu.CompilerParams(vmem_limit_bytes=26 * 1024 * 1024),
     )(tokens, tokens, tokens, tokens, ids, *got, rel_index, bias_table, *weights, inner)
 
 
@@ -675,9 +804,12 @@
         norm1_gain.reshape(1, C), w_qkv, w_proj, norm2_gain.reshape(1, C), w_up, w_down,
         merge_gain.reshape(1, 4 * C), w_merge,
     )
+    bias_table = bias_table.T
+    tokens = pltpu.with_memory_space_constraint(tokens, pltpu.HBM)
     ids, top, bottom = pack_rows(tokens, regions)
     above, below = moved(bottom, "row", 1), moved(top, "row", -1)
     inner = interior(tokens, ids, rel_index, bias_table, weights, 0, EARLY)
+    inner = pltpu.with_memory_space_constraint(inner, pltpu.HBM)
     to_left, to_right, token = pack_cols(tokens, above, below, ids, inner)
     from_left, from_right = moved(to_right, "col", 1), moved(to_left, "col", -1)
     inner = interior(

time: 94.9 us -> 89.6 us (0.944)
  Pallas kernels: 80 us -> 76.6 us
  local copies, waits for them, and re-layouts: 3.37 us -> 0.92 us
    pallas_call x2, Pallas kernels: 55.6 us -> 52.6 us  [interior(): pl.pallas_call(functools.partial(interior_kernel, first, total), grid=(to...]
    unnamed x11 -> x22, local copies, waits for them, and re-layouts: 3.37 us -> 0.92 us
  transfers between devices with their start and end apart: 4 -> 4, of which waited for: 0 -> 0; matrix products, arithmetic and copies ran while one was open for 1% -> 0% of each run, Pallas kernels for 59% -> 59%
where the time goes in v3:
time: 89.6 us; the launch traced here: 88.9 us
  Pallas kernels  76.6 us (85%)
  starting transfers between devices  11 us (12%)
  local copies, waits for them, and re-layouts  0.92 us (1%)
    pallas_call x2, Pallas kernels, interior(): pl.pallas_call(functools.partial(interior_kernel, first, total), grid=(to...  52.6 us
    pallas_call x1, Pallas kernels, border(): pl.pallas_call(border_kernel, grid=(5,), out_shape=jax.ShapeDtypeStruct((...  21.2 us
    ppermute x4, starting transfers between devices, moved(): lax.ppermute(value, axis, [(i, (i + by) % size) for i in range(size)])  11 us
  transfers between devices with their start and end apart: 4, of which 0 were waited for; matrix products, arithmetic and copies ran while one was open for 0% of the time, Pallas kernels for 59%

profile of v3, /device:TPU:0, one launch (start us, length us, event | category | flops | bytes accessed | tf_op | source)
XLA Modules:
  0.0 88.9 jit_solution(8645437575165444900)
XLA Ops:
  0.0 0.0 copy-start.4
  0.0 0.0 copy-start.3
  0.0 0.0 copy-start.5
  0.0 0.0 copy-start.1
  0.0 0.0 copy-start.2
  0.0 0.0 copy-start.6
  0.0 0.9 copy-done.6
  0.9 0.0 copy-start
  0.9 0.0 copy-start.10
  0.9 1.1 %shard_map.118 = (s32[8,128]{1,0:T(8,128)S(1)}, bf16[528,128]{1,0:T(8,128)(2,1)S(1)}, bf16[528,128]{1,0:T(8,128)(2,1)S(1)}) custom-call(f32[128,128,128]{2,1,0:T(8,128)} %refs_3_.1, f32[128,128,128]{2,1,0:T(8,128)} %refs_3_.1, s32[128,128]{1,0:T(8,128)S(1)} %copy-done.6), custom_call_target="tpu_custom_call" | custom-call | tf_op jit(solution)/shard_map/pallas_call | solution.py:437
  2.0 0.1 collective-permute-start
  2.1 3.8 %collective-permute-start.1 = (bf16[528,128]{1,0:T(8,128)(2,1)S(1)}, bf16[528,128]{1,0:T(8,128)(2,1)S(1)}, u32[]{:S(2)}, u32[]{:S(2)}) collective-permute-start(bf16[528,128]{1,0:T(8,128)(2,1)S(1)} %get-tuple-element.13), channel_id=1, source_target_pairs={{0,240},{16,0},{32,16},{48,32},{64,48},{80,64},{96,80},{112,96},{1... | collective-permute-start | bytes 405512 | tf_op jit(solution)/shard_map/ppermute | solution.py:500
  6.0 0.0 copy-done.4
  6.0 0.0 copy-done.3
  6.0 0.0 copy-done.5
  6.0 0.0 copy-done.1
  6.0 0.0 copy-done.2
  6.0 0.0 copy-done
  6.0 0.0 copy-done.7
  6.0 0.0 copy-done.8
  6.0 0.0 copy-done.9
  6.0 0.0 copy-done.10
  6.0 12.8 %shard_map.119.after_ref.refs_8_ = bf16[64,64,256]{2,1,0:T(8,128)(2,1)} custom-call(f32[128,128,128]{2,1,0:T(8,128)} %refs_3_.1, f32[128,128,128]{2,1,0:T(8,128)} %refs_3_.1, s32[8,128]{1,0:T(8,128)S(1)} %get-tuple-element.11.ids_ref.refs_4_, s32[64,64]{1,0:T(8,128)S(1)} %copy-done.4, f32[4,225]{1,0:T(4,128)S(1)} %bitcast.4, f32[1,128]{1,0:T(1,128)S(1)} %bitcast.10, ...), custom_call_target="tpu_custom_call" | custom-call | tf_op jit(solution)/shard_map/pallas_call | solution.py:369
  18.9 0.0 collective-permute-done.above_any.refs_5_
  18.9 0.0 collective-permute-done.1.below_any.refs_6_
  18.9 1.7 %shard_map.120 = (bf16[592,128]{1,0:T(8,128)(2,1)S(1)}, bf16[592,128]{1,0:T(8,128)(2,1)S(1)}, f32[8,128]{1,0:T(8,128)S(1)}) custom-call(f32[128,128,128]{2,1,0:T(8,128)} %refs_3_.1, f32[128,128,128]{2,1,0:T(8,128)} %refs_3_.1, bf16[528,128]{1,0:T(8,128)(2,1)S(1)} %collective-permute-done.above_any.refs_5_, ...), custom_call_target="tpu_custom_call" | custom-call | tf_op jit(solution)/shard_map/pallas_call | solution.py:479
  20.6 1.5 %collective-permute-start.2 = (bf16[592,128]{1,0:T(8,128)(2,1)S(1)}, bf16[592,128]{1,0:T(8,128)(2,1)S(1)}, u32[]{:S(2)}, u32[]{:S(2)}) collective-permute-start(bf16[592,128]{1,0:T(8,128)(2,1)S(1)} %get-tuple-element.14), channel_id=1, source_target_pairs={{0,1},{1,2},{2,3},{3,4},{4,5},{5,6},{6,7},{7,8},{8,9},{9,10},{10,1... | collective-permute-start | bytes 454664 | tf_op jit(solution)/shard_map/ppermute | solution.py:500
  22.1 5.6 %collective-permute-start.3 = (bf16[592,128]{1,0:T(8,128)(2,1)S(1)}, bf16[592,128]{1,0:T(8,128)(2,1)S(1)}, u32[]{:S(2)}, u32[]{:S(2)}) collective-permute-start(bf16[592,128]{1,0:T(8,128)(2,1)S(1)} %get-tuple-element.15), channel_id=1, source_target_pairs={{0,15},{1,0},{2,1},{3,2},{4,3},{5,4},{6,5},{7,6},{8,7},{9,8},{10,9... | collective-permute-start | bytes 454664 | tf_op jit(solution)/shard_map/ppermute | solution.py:500
  27.7 39.8 %shard_map.121.refs_19_ = bf16[64,64,256]{2,1,0:T(8,128)(2,1)} custom-call(f32[128,128,128]{2,1,0:T(8,128)} %refs_3_.1, f32[128,128,128]{2,1,0:T(8,128)} %refs_3_.1, s32[8,128]{1,0:T(8,128)S(1)} %get-tuple-element.11.ids_ref.refs_4_, s32[64,64]{1,0:T(8,128)S(1)} %copy-done.4, f32[4,225]{1,0:T(4,128)S(1)} %bitcast.5, ...), custom_call_target="tpu_custom_call", output_to_operand_aliasing={{}: (13, {})} | custom-call | tf_op jit(solution)/shard_map/pallas_call | solution.py:369
  67.5 0.0 collective-permute-done.2.refs_7_
  67.5 0.0 collective-permute-done.3.refs_8_
  67.5 21.2 %shard_map.122 = bf16[64,64,256]{2,1,0:T(8,128)(2,1)} custom-call(f32[128,128,128]{2,1,0:T(8,128)} %refs_3_.1, f32[128,128,128]{2,1,0:T(8,128)} %refs_3_.1, f32[128,128,128]{2,1,0:T(8,128)} %refs_3_.1, f32[128,128,128]{2,1,0:T(8,128)} %refs_3_.1, s32[8,128]{1,0:T(8,128)S(1)} %get-tuple-element.11.ids_ref.refs_4_, ...), custom_call_target="tpu_custom_call", output_to_operand_aliasing={{}: (19, {})} | custom-call | tf_op jit(solution)/shard_map/pallas_call | solution.py:753
  (3 shorter events, 0.0 us)
Async XLA Ops:
  0.0 6.0 %copy-start.4 = (s32[64,64]{1,0:T(8,128)S(1)}, s32[64,64]{1,0:T(8,128)}, u32[]{:S(2)}) copy-start(s32[64,64]{1,0:T(8,128)} %refs_9_.1) | copy-start | bytes 49156
  0.0 6.0 %copy-start.3 = (bf16[128,384]{1,0:T(8,128)(2,1)S(1)}, bf16[128,384]{1,0:T(8,128)(2,1)}, u32[]{:S(2)}) copy-start(bf16[128,384]{1,0:T(8,128)(2,1)} %refs_12_.1) | copy-start | bytes 294916
  0.0 6.0 %copy-start.5 = (bf16[128,128]{1,0:T(8,128)(2,1)S(1)}, bf16[128,128]{1,0:T(8,128)(2,1)}, u32[]{:S(2)}) copy-start(bf16[128,128]{1,0:T(8,128)(2,1)} %refs_13_.1) | copy-start | bytes 98308
  0.0 6.0 %copy-start.1 = (bf16[128,512]{1,0:T(8,128)(2,1)S(1)}, bf16[128,512]{1,0:T(8,128)(2,1)}, u32[]{:S(2)}) copy-start(bf16[128,512]{1,0:T(8,128)(2,1)} %refs_15_.1) | copy-start | bytes 393220
  0.0 6.0 %copy-start.2 = (bf16[512,128]{1,0:T(8,128)(2,1)S(1)}, bf16[512,128]{1,0:T(8,128)(2,1)}, u32[]{:S(2)}) copy-start(bf16[512,128]{1,0:T(8,128)(2,1)} %refs_16_.1) | copy-start | bytes 393220
  0.0 0.9 %copy-start.6 = (s32[128,128]{1,0:T(8,128)S(1)}, s32[128,128]{1,0:T(8,128)}, u32[]{:S(2)}) copy-start(s32[128,128]{1,0:T(8,128)} %regions_ref.1) | copy-start | bytes 196612
  0.9 5.1 %copy-start = (bf16[512,256]{1,0:T(8,128)(2,1)S(1)}, bf16[512,256]{1,0:T(8,128)(2,1)}, u32[]{:S(2)}) copy-start(bf16[512,256]{1,0:T(8,128)(2,1)} %refs_18_.1) | copy-start | bytes 786436
  0.9 5.1 %copy-start.7 = (f32[225,4]{0,1:T(4,128)S(1)}, f32[225,4]{0,1:T(4,128)}, u32[]{:S(2)}) copy-start(f32[225,4]{0,1:T(4,128)} %param.15) | copy-start | bytes 10804
  0.9 5.1 %copy-start.8 = (f32[512]{0:T(512)S(1)}, f32[512]{0:T(512)}, u32[]{:S(2)}) copy-start(f32[512]{0:T(512)} %param.22) | copy-start | bytes 6148
  0.9 5.1 %copy-start.9 = (f32[128]{0:T(128)S(1)}, f32[128]{0:T(128)}, u32[]{:S(2)}) copy-start(f32[128]{0:T(128)} %param.16) | copy-start | bytes 1540
  0.9 5.1 %copy-start.10 = (f32[128]{0:T(128)S(1)}, f32[128]{0:T(128)}, u32[]{:S(2)}) copy-start(f32[128]{0:T(128)} %param.19) | copy-start | bytes 1540
  2.0 16.8 %collective-permute-start = (bf16[528,128]{1,0:T(8,128)(2,1)S(1)}, bf16[528,128]{1,0:T(8,128)(2,1)S(1)}, u32[]{:S(2)}, u32[]{:S(2)}) collective-permute-start(bf16[528,128]{1,0:T(8,128)(2,1)S(1)} %get-tuple-element.12), channel_id=1, source_target_pairs={{0,16},{16,32},{32,48},{48,64},{64,80},{80,96},{96,112},{112,128},... | collective-permute-start | bytes 405512 | tf_op jit(solution)/shard_map/ppermute | solution.py:500
  2.1 16.7 %collective-permute-start.1 = (bf16[528,128]{1,0:T(8,128)(2,1)S(1)}, bf16[528,128]{1,0:T(8,128)(2,1)S(1)}, u32[]{:S(2)}, u32[]{:S(2)}) collective-permute-start(bf16[528,128]{1,0:T(8,128)(2,1)S(1)} %get-tuple-element.13), channel_id=1, source_target_pairs={{0,240},{16,0},{32,16},{48,32},{64,48},{80,64},{96,80},{112,96},{1... | collective-permute-start | bytes 405512 | tf_op jit(solution)/shard_map/ppermute | solution.py:500
  20.6 46.9 %collective-permute-start.2 = (bf16[592,128]{1,0:T(8,128)(2,1)S(1)}, bf16[592,128]{1,0:T(8,128)(2,1)S(1)}, u32[]{:S(2)}, u32[]{:S(2)}) collective-permute-start(bf16[592,128]{1,0:T(8,128)(2,1)S(1)} %get-tuple-element.14), channel_id=1, source_target_pairs={{0,1},{1,2},{2,3},{3,4},{4,5},{5,6},{6,7},{7,8},{8,9},{9,10},{10,1... | collective-permute-start | bytes 454664 | tf_op jit(solution)/shard_map/ppermute | solution.py:500
  22.1 45.4 %collective-permute-start.3 = (bf16[592,128]{1,0:T(8,128)(2,1)S(1)}, bf16[592,128]{1,0:T(8,128)(2,1)S(1)}, u32[]{:S(2)}, u32[]{:S(2)}) collective-permute-start(bf16[592,128]{1,0:T(8,128)(2,1)S(1)} %get-tuple-element.15), channel_id=1, source_target_pairs={{0,15},{1,0},{2,1},{3,2},{4,3},{5,4},{6,5},{7,6},{8,7},{9,8},{10,9... | collective-permute-start | bytes 454664 | tf_op jit(solution)/shard_map/ppermute | solution.py:500

commit v4 on v3

--- a/solution.py
+++ b/solution.py
@@ -235,7 +235,7 @@
 
 PIECE = 256
 QPIECE = 256
-LAG = 1
+LAG = 2
 
 
 def merge(load_parts, store, w):
@@ -806,6 +806,7 @@
     )
     bias_table = bias_table.T
     tokens = pltpu.with_memory_space_constraint(tokens, pltpu.HBM)
+    regions = pltpu.with_memory_space_constraint(regions, pltpu.HBM)
     ids, top, bottom = pack_rows(tokens, regions)
     above, below = moved(bottom, "row", 1), moved(top, "row", -1)
     inner = interior(tokens, ids, rel_index, bias_table, weights, 0, EARLY)

time: 89.6 us -> 88.4 us (0.987)
  transfers between devices with their start and end apart: 4 -> 4, of which waited for: 0 -> 0; matrix products, arithmetic and copies ran while one was open for 0% -> 0% of each run, Pallas kernels for 59% -> 60%
where the time goes in v4:
time: 88.4 us; the launch traced here: 87.7 us
  Pallas kernels  76.3 us (86%)
  starting transfers between devices  11 us (12%)
    pallas_call x2, Pallas kernels, interior(): pl.pallas_call(functools.partial(interior_kernel, first, total), grid=(to...  52.8 us
    pallas_call x1, Pallas kernels, border(): pl.pallas_call(border_kernel, grid=(5,), out_shape=jax.ShapeDtypeStruct((...  20.6 us
    ppermute x4, starting transfers between devices, moved(): lax.ppermute(value, axis, [(i, (i + by) % size) for i in range(size)])  11 us
  transfers between devices with their start and end apart: 4, of which 0 were waited for; matrix products, arithmetic and copies ran while one was open for 0% of the time, Pallas kernels for 60%

profile of v4, /device:TPU:0, one launch (start us, length us, event | category | flops | bytes accessed | tf_op | source)
XLA Modules:
  0.0 87.7 jit_solution(8347436438651982462)
XLA Ops:
  0.0 0.0 copy-start.4
  0.0 0.0 copy-start.6
  0.0 0.0 copy-start.8
  0.0 0.0 copy-start.3
  0.0 0.0 copy-start.9
  0.0 0.0 copy-start.1
  0.0 0.0 copy-start.2
  0.0 0.0 copy-start.7
  0.1 0.0 copy-start
  0.1 1.2 %shard_map.118 = (s32[8,128]{1,0:T(8,128)S(1)}, bf16[528,128]{1,0:T(8,128)(2,1)S(1)}, bf16[528,128]{1,0:T(8,128)(2,1)S(1)}) custom-call(f32[128,128,128]{2,1,0:T(8,128)} %refs_3_.1, f32[128,128,128]{2,1,0:T(8,128)} %refs_3_.1, s32[128,128]{1,0:T(8,128)} %regions_ref.1), custom_call_target="tpu_custom_call" | custom-call | tf_op jit(solution)/shard_map/pallas_call | solution.py:437
  1.3 0.1 collective-permute-start
  1.4 3.8 %collective-permute-start.1 = (bf16[528,128]{1,0:T(8,128)(2,1)S(1)}, bf16[528,128]{1,0:T(8,128)(2,1)S(1)}, u32[]{:S(2)}, u32[]{:S(2)}) collective-permute-start(bf16[528,128]{1,0:T(8,128)(2,1)S(1)} %get-tuple-element.13), channel_id=1, source_target_pairs={{0,240},{16,0},{32,16},{48,32},{64,48},{80,64},{96,80},{112,96},{1... | collective-permute-start | bytes 405512 | tf_op jit(solution)/shard_map/ppermute | solution.py:500
  5.2 0.0 copy-done.4
  5.2 0.0 copy-done.6
  5.2 0.0 copy-done.8
  5.2 0.0 copy-done.3
  5.2 0.0 copy-done.5
  5.2 0.0 copy-done.9
  5.2 0.0 copy-done.1
  5.3 0.0 copy-done.2
  5.3 0.0 copy-done.7
  5.3 0.0 copy-done
  5.3 12.9 %shard_map.119.after_ref.refs_8_ = bf16[64,64,256]{2,1,0:T(8,128)(2,1)} custom-call(f32[128,128,128]{2,1,0:T(8,128)} %refs_3_.1, f32[128,128,128]{2,1,0:T(8,128)} %refs_3_.1, s32[8,128]{1,0:T(8,128)S(1)} %get-tuple-element.11.ids_ref.refs_4_, s32[64,64]{1,0:T(8,128)S(1)} %copy-done.4, f32[4,225]{1,0:T(4,128)S(1)} %bitcast.4, f32[1,128]{1,0:T(1,128)S(1)} %bitcast.10, ...), custom_call_target="tpu_custom_call" | custom-call | tf_op jit(solution)/shard_map/pallas_call | solution.py:369
  18.1 0.0 collective-permute-done.above_any.refs_5_
  18.1 0.0 collective-permute-done.1.below_any.refs_6_
  18.1 1.7 %shard_map.120 = (bf16[592,128]{1,0:T(8,128)(2,1)S(1)}, bf16[592,128]{1,0:T(8,128)(2,1)S(1)}, f32[8,128]{1,0:T(8,128)S(1)}) custom-call(f32[128,128,128]{2,1,0:T(8,128)} %refs_3_.1, f32[128,128,128]{2,1,0:T(8,128)} %refs_3_.1, bf16[528,128]{1,0:T(8,128)(2,1)S(1)} %collective-permute-done.above_any.refs_5_, ...), custom_call_target="tpu_custom_call" | custom-call | tf_op jit(solution)/shard_map/pallas_call | solution.py:479
  19.8 1.6 %collective-permute-start.2 = (bf16[592,128]{1,0:T(8,128)(2,1)S(1)}, bf16[592,128]{1,0:T(8,128)(2,1)S(1)}, u32[]{:S(2)}, u32[]{:S(2)}) collective-permute-start(bf16[592,128]{1,0:T(8,128)(2,1)S(1)} %get-tuple-element.14), channel_id=1, source_target_pairs={{0,1},{1,2},{2,3},{3,4},{4,5},{5,6},{6,7},{7,8},{8,9},{9,10},{10,1... | collective-permute-start | bytes 454664 | tf_op jit(solution)/shard_map/ppermute | solution.py:500
  21.4 5.6 %collective-permute-start.3 = (bf16[592,128]{1,0:T(8,128)(2,1)S(1)}, bf16[592,128]{1,0:T(8,128)(2,1)S(1)}, u32[]{:S(2)}, u32[]{:S(2)}) collective-permute-start(bf16[592,128]{1,0:T(8,128)(2,1)S(1)} %get-tuple-element.15), channel_id=1, source_target_pairs={{0,15},{1,0},{2,1},{3,2},{4,3},{5,4},{6,5},{7,6},{8,7},{9,8},{10,9... | collective-permute-start | bytes 454664 | tf_op jit(solution)/shard_map/ppermute | solution.py:500
  27.0 39.9 %shard_map.121.refs_19_ = bf16[64,64,256]{2,1,0:T(8,128)(2,1)} custom-call(f32[128,128,128]{2,1,0:T(8,128)} %refs_3_.1, f32[128,128,128]{2,1,0:T(8,128)} %refs_3_.1, s32[8,128]{1,0:T(8,128)S(1)} %get-tuple-element.11.ids_ref.refs_4_, s32[64,64]{1,0:T(8,128)S(1)} %copy-done.4, f32[4,225]{1,0:T(4,128)S(1)} %bitcast.5, ...), custom_call_target="tpu_custom_call", output_to_operand_aliasing={{}: (13, {})} | custom-call | tf_op jit(solution)/shard_map/pallas_call | solution.py:369
  66.9 0.0 collective-permute-done.2.refs_7_
  66.9 0.0 collective-permute-done.3.refs_8_
  66.9 20.6 %shard_map.122 = bf16[64,64,256]{2,1,0:T(8,128)(2,1)} custom-call(f32[128,128,128]{2,1,0:T(8,128)} %refs_3_.1, f32[128,128,128]{2,1,0:T(8,128)} %refs_3_.1, f32[128,128,128]{2,1,0:T(8,128)} %refs_3_.1, f32[128,128,128]{2,1,0:T(8,128)} %refs_3_.1, s32[8,128]{1,0:T(8,128)S(1)} %get-tuple-element.11.ids_ref.refs_4_, ...), custom_call_target="tpu_custom_call", output_to_operand_aliasing={{}: (19, {})} | custom-call | tf_op jit(solution)/shard_map/pallas_call | solution.py:753
  (1 shorter events, 0.0 us)
Async XLA Ops:
  0.0 5.2 %copy-start.4 = (s32[64,64]{1,0:T(8,128)S(1)}, s32[64,64]{1,0:T(8,128)}, u32[]{:S(2)}) copy-start(s32[64,64]{1,0:T(8,128)} %refs_9_.1) | copy-start | bytes 49156
  0.0 5.2 %copy-start.6 = (f32[225,4]{0,1:T(4,128)S(1)}, f32[225,4]{0,1:T(4,128)}, u32[]{:S(2)}) copy-start(f32[225,4]{0,1:T(4,128)} %param.15) | copy-start | bytes 10804
  0.0 5.2 %copy-start.8 = (f32[128]{0:T(128)S(1)}, f32[128]{0:T(128)}, u32[]{:S(2)}) copy-start(f32[128]{0:T(128)} %param.16) | copy-start | bytes 1540
  0.0 5.2 %copy-start.3 = (bf16[128,384]{1,0:T(8,128)(2,1)S(1)}, bf16[128,384]{1,0:T(8,128)(2,1)}, u32[]{:S(2)}) copy-start(bf16[128,384]{1,0:T(8,128)(2,1)} %refs_12_.1) | copy-start | bytes 294916
  0.0 5.2 %copy-start.5 = (bf16[128,128]{1,0:T(8,128)(2,1)S(1)}, bf16[128,128]{1,0:T(8,128)(2,1)}, u32[]{:S(2)}) copy-start(bf16[128,128]{1,0:T(8,128)(2,1)} %refs_13_.1) | copy-start | bytes 98308
  0.0 5.2 %copy-start.9 = (f32[128]{0:T(128)S(1)}, f32[128]{0:T(128)}, u32[]{:S(2)}) copy-start(f32[128]{0:T(128)} %param.19) | copy-start | bytes 1540
  0.0 5.2 %copy-start.1 = (bf16[128,512]{1,0:T(8,128)(2,1)S(1)}, bf16[128,512]{1,0:T(8,128)(2,1)}, u32[]{:S(2)}) copy-start(bf16[128,512]{1,0:T(8,128)(2,1)} %refs_15_.1) | copy-start | bytes 393220
  0.0 5.2 %copy-start.2 = (bf16[512,128]{1,0:T(8,128)(2,1)S(1)}, bf16[512,128]{1,0:T(8,128)(2,1)}, u32[]{:S(2)}) copy-start(bf16[512,128]{1,0:T(8,128)(2,1)} %refs_16_.1) | copy-start | bytes 393220
  0.0 5.2 %copy-start.7 = (f32[512]{0:T(512)S(1)}, f32[512]{0:T(512)}, u32[]{:S(2)}) copy-start(f32[512]{0:T(512)} %param.22) | copy-start | bytes 6148
  0.1 5.2 %copy-start = (bf16[512,256]{1,0:T(8,128)(2,1)S(1)}, bf16[512,256]{1,0:T(8,128)(2,1)}, u32[]{:S(2)}) copy-start(bf16[512,256]{1,0:T(8,128)(2,1)} %refs_18_.1) | copy-start | bytes 786436
  1.3 16.9 %collective-permute-start = (bf16[528,128]{1,0:T(8,128)(2,1)S(1)}, bf16[528,128]{1,0:T(8,128)(2,1)S(1)}, u32[]{:S(2)}, u32[]{:S(2)}) collective-permute-start(bf16[528,128]{1,0:T(8,128)(2,1)S(1)} %get-tuple-element.12), channel_id=1, source_target_pairs={{0,16},{16,32},{32,48},{48,64},{64,80},{80,96},{96,112},{112,128},... | collective-permute-start | bytes 405512 | tf_op jit(solution)/shard_map/ppermute | solution.py:500
  1.4 16.8 %collective-permute-start.1 = (bf16[528,128]{1,0:T(8,128)(2,1)S(1)}, bf16[528,128]{1,0:T(8,128)(2,1)S(1)}, u32[]{:S(2)}, u32[]{:S(2)}) collective-permute-start(bf16[528,128]{1,0:T(8,128)(2,1)S(1)} %get-tuple-element.13), channel_id=1, source_target_pairs={{0,240},{16,0},{32,16},{48,32},{64,48},{80,64},{96,80},{112,96},{1... | collective-permute-start | bytes 405512 | tf_op jit(solution)/shard_map/ppermute | solution.py:500
  19.8 47.0 %collective-permute-start.2 = (bf16[592,128]{1,0:T(8,128)(2,1)S(1)}, bf16[592,128]{1,0:T(8,128)(2,1)S(1)}, u32[]{:S(2)}, u32[]{:S(2)}) collective-permute-start(bf16[592,128]{1,0:T(8,128)(2,1)S(1)} %get-tuple-element.14), channel_id=1, source_target_pairs={{0,1},{1,2},{2,3},{3,4},{4,5},{5,6},{6,7},{7,8},{8,9},{9,10},{10,1... | collective-permute-start | bytes 454664 | tf_op jit(solution)/shard_map/ppermute | solution.py:500
  21.4 45.5 %collective-permute-start.3 = (bf16[592,128]{1,0:T(8,128)(2,1)S(1)}, bf16[592,128]{1,0:T(8,128)(2,1)S(1)}, u32[]{:S(2)}, u32[]{:S(2)}) collective-permute-start(bf16[592,128]{1,0:T(8,128)(2,1)S(1)} %get-tuple-element.15), channel_id=1, source_target_pairs={{0,15},{1,0},{2,1},{3,2},{4,3},{5,4},{6,5},{7,6},{8,7},{9,8},{10,9... | collective-permute-start | bytes 454664 | tf_op jit(solution)/shard_map/ppermute | solution.py:500
